TPU v7x, 32 devices: a whole 2x2x4 slice. The times are simulated.
32 devices in a mesh: front: 4 (over z), lat: 8 (over y, x, core).
Axes of the slice: x: 2, y: 2, z: 4, core: 2. Of those that a mesh axis runs over, the one named last changes fastest.
Arguments:
- samples: float32 [64, 128, 128], P('front', 'lat'), may hold values from -6 to 6
- reaction: float32 [64, 128], P('front', 'lat'), may hold values from 0.5 to 2
- weight_x: float32 [64, 128], P('front', 'lat'), may hold values from 0.2 to 1
- weight_y: float32 [64, 128], P('front', 'lat'), may hold values from 0.2 to 1
- inverses: float32 [4, 16, 128, 128], P('front', 'lat'), may hold values from -0.3 to 0.4
- couplings: float32 [4, 16, 128, 128], P('front', 'lat'), may hold values from -12 to 12
Outputs:
- whitened: float32 [64, 128, 128], P('front', 'lat')
- gradients: float32 [3, 64, 128], P(None, 'front', 'lat')
All inputs are finite; a program needn't handle non-finite values.
Results may differ from a plain program's by a relative error of at most 0.0003.
Values sent between devices are 32-bit elements; how exact they have to be, the bound alone decides.
A program may use at most 192 MiB of HBM per device.

v0:
```python
import jax
import jax.numpy as jnp
from jax import lax
from jax.sharding import PartitionSpec as P


def prefix(array, axis, combine, identity, reverse):
    length, here = (lax.axis_size(axis), lax.axis_index(axis))
    everything = jax.tree.map(lambda part: lax.all_gather(part, axis), array)
    start = jax.tree.map(
        lambda part, zero: jnp.broadcast_to(jnp.asarray(zero, part.dtype), part.shape),
        array,
        identity,
    )

    def hop(k, before):
        at = length - 1 - k if reverse else k
        reached = at > here if reverse else at < here
        new = combine(before, jax.tree.map(lambda part: part[at], everything))
        return jax.tree.map(lambda a, b: jnp.where(reached, a, b), new, before)

    return lax.fori_loop(0, length, hop, start)


def extended(array, sides, width):
    for axis, dim in sides:
        size, length = (lax.axis_size(axis), array.shape[dim])
        up = [(i, (i + 1) % size) for i in range(size - 1)]
        down = [(j, i) for i, j in up]
        last = lax.slice_in_dim(array, length - width, length, axis=dim)
        initial = lax.slice_in_dim(array, 0, width, axis=dim)
        before = lax.ppermute(last, axis, up)
        after = lax.ppermute(initial, axis, down)
        array = jnp.concatenate([before, array, after], axis=dim)
    return array


def matmul(left, right):
    return jnp.dot(left, right, precision=lax.Precision.HIGHEST, preferred_element_type=jnp.float32)


def left_transpose_product(left, right):
    return lax.dot_general(
        left,
        right,
        (((0,), (0,)), ((), ())),
        precision=lax.Precision.HIGHEST,
        preferred_element_type=jnp.float32,
    )


def compose(earlier, later):
    return (matmul(later[0], earlier[0]), matmul(later[0], earlier[1]) + later[1])


def chain_prefix(maps, backward):
    width, count = maps[1].shape
    ident = (jnp.eye(width, dtype=jnp.float32), jnp.zeros((width, count), jnp.float32))
    if backward:
        result = prefix(maps, ("front", "lat"), compose, ident, True)
    else:
        result = prefix(maps, ("front", "lat"), compose, ident, False)
    return result[1]


def body(samples, reaction, weight_x, weight_y, inverses, couplings):
    tile_along_x, tile_y, count = samples.shape
    panels = inverses.shape[1]
    width = inverses.shape[3]
    padded = extended(samples, (("front", 0), ("lat", 1)), 1)
    lap_x = 2.0 * samples - padded[:-2, 1:-1] - padded[2:, 1:-1]
    lap_y = 2.0 * samples - padded[1:-1, :-2] - padded[1:-1, 2:]
    resid = (
        reaction[:, :, None] * samples + weight_x[:, :, None] * lap_x + weight_y[:, :, None] * lap_y
    )
    source_vectors = resid.reshape(panels, width, count)
    reciprocal_pieces = inverses.reshape(panels, width, width)
    lower_band_coupling = couplings.reshape(panels, width, width)
    eye = jnp.eye(width, dtype=jnp.float32)
    running_carry = jnp.zeros((width, count), jnp.float32)
    carried = eye
    local_values = []
    local_maps = []
    for index in range(panels):
        running_carry = matmul(
            reciprocal_pieces[index],
            source_vectors[index] - matmul(lower_band_coupling[index], running_carry),
        )
        carried = -matmul(reciprocal_pieces[index], matmul(lower_band_coupling[index], carried))
        local_values.append(running_carry)
        local_maps.append(carried)
    incoming = chain_prefix((carried, running_carry), False)
    unknown_answer = [
        local_values[index] + matmul(local_maps[index], incoming) for index in range(panels)
    ]
    running_carry = jnp.zeros((width, count), jnp.float32)
    carried = eye
    adjoint_values = [None] * panels
    adjoint_maps = [None] * panels
    for index in reversed(range(panels)):
        first = left_transpose_product(
            reciprocal_pieces[index], unknown_answer[index] - running_carry
        )
        mapped = -left_transpose_product(reciprocal_pieces[index], carried)
        adjoint_values[index] = first
        adjoint_maps[index] = mapped
        running_carry = left_transpose_product(lower_band_coupling[index], first)
        carried = left_transpose_product(lower_band_coupling[index], mapped)
    incoming = chain_prefix((carried, running_carry), True)
    reverse_mode_pieces = jnp.stack(
        [adjoint_values[index] + matmul(adjoint_maps[index], incoming) for index in range(panels)]
    )
    whitened = reverse_mode_pieces.reshape(tile_along_x, tile_y, count)
    gradients = jnp.stack(
        [
            jnp.mean(whitened * samples, axis=2),
            jnp.mean(whitened * lap_x, axis=2),
            jnp.mean(whitened * lap_y, axis=2),
        ]
    )
    return (whitened, gradients)


def solution(mesh):
    placed = (
        P("front", "lat", None),
        P("front", "lat"),
        P("front", "lat"),
        P("front", "lat"),
        P("front", "lat", None, None),
        P("front", "lat", None, None),
    )
    return jax.shard_map(
        body,
        mesh=mesh,
        in_specs=placed,
        out_specs=(P("front", "lat", None), P(None, "front", "lat")),
        check_vma=False,
    )
```

profile of v0, /device:TPU:0, one launch (start us, length us, event | category | flops | bytes accessed | tf_op | source)
XLA Modules:
  0.0 294.2 jit_solution(2181341815415806913)
XLA Ops:
  7.2 1.1 fusion.43
  8.4 1.1 convolution_negate_fusion.3
  9.5 1.1 fusion.33
  10.6 1.7 convolution_negate_fusion.2
  13.1 4.9 %collective-permute-start = (f32[1,16,128]{2,1,0:T(8,128)S(1)}, f32[1,16,128]{2,1,0:T(8,128)S(1)}, u32[]{:S(2)}, u32[]{:S(2)}) collective-permute-start(f32[1,16,128]{2,1,0:T(8,128)S(1)} %get-tuple-element.303), channel_id=1, source_target_pairs={{0,8},{8,16},{16,24},{1,9},{9,17},{17,25},{2,10},{10,18},{18,26},{... | collective-permute-start | bytes 24584 | tf_op jit(solution)/shard_map/ppermute | solution.py:32
  18.0 1.3 collective-permute-start.1
  20.3 3.3 %collective-permute-done.1 = f32[1,16,128]{2,1,0:T(8,128)S(1)} collective-permute-done((f32[1,16,128]{2,1,0:T(8,128)S(1)}, f32[1,16,128]{2,1,0:T(8,128)S(1)}, u32[]{:S(2)}, u32[]{:S(2)}) %collective-permute-start.1) | collective-permute-done | bytes 8224 | tf_op jit(solution)/shard_map/ppermute | solution.py:33
  23.6 1.3 collective-permute-start.2
  24.9 1.3 collective-permute-start.3
  27.2 2.5 collective-permute-done.3
  29.7 1.2 multiply_add_fusion
  31.0 1.1 fusion.39
  35.0 36.9 %all-gather.9.cloned.1.call-done = f32[4096,128]{0,1:T(8,128)} async-done(((f32[128,128]{0,1:T(8,128)}), f32[4096,128]{0,1:T(8,128)}) %all-gather.9.cloned.1.call-update) | async-done | bytes 2097168 | tf_op jit(solution)/shard_map/all_gather | solution.py:9
  71.9 1.9 copy.12
  73.8 56.6 %all-gather.11.cloned.1.call-done = f32[4096,128]{0,1:T(8,128)} async-done(((f32[128,128]{0,1:T(8,128)}), f32[4096,128]{0,1:T(8,128)}) %all-gather.11.cloned.1.call-update) | async-done | bytes 2097168 | tf_op jit(solution)/shard_map/all_gather | solution.py:9
  130.4 2.9 copy.13
  133.3 35.0 %while.30 = (s32[]{:T(128)}, f32[128,128]{1,0:T(8,128)S(1)}, s32[]{:T(128)}, f32[32,128,128]{2,1,0:T(8,128)S(1)}, f32[32,128,128]{2,1,0:T(8,128)}, /*index=5*/s32[]{:T(128)}, s32[]{:T(128)}) while((s32[]{:T(128)}, f32[128,128]{1,0:T(8,128)S(1)}, s32[]{:T(128)}, f32[32,128,128]{2,1,0:T(8,128)S(1)}, f32[32,128,128]{2,1,0:T(8,128)}, ...), condition=%wide.region_2.3_spmd.clone, body=%wide.region_1.2_spmd.clone.sunk | while | flops 25231364 | bytes 461407 | solution.py:22
  133.3 1.1 fusion.94
  134.5 1.1 fusion.94
  136.7 1.1 fusion.94
  137.7 1.1 fusion.94
  139.9 1.1 fusion.94
  141.0 1.1 fusion.94
  145.4 1.1 fusion.94
  147.6 1.1 fusion.94
  149.8 1.1 fusion.94
  152.0 1.1 fusion.94
  153.1 1.1 fusion.94
  154.2 1.1 fusion.94
  156.4 1.1 fusion.94
  158.6 1.1 fusion.94
  159.6 1.1 fusion.94
  160.7 1.1 fusion.94
  162.9 1.1 fusion.94
  165.1 1.1 fusion.94
  166.2 1.1 fusion.94
  167.3 1.1 fusion.94
  170.8 18.9 %all-gather.13.cloned.1.call-done = f32[4096,128]{0,1:T(8,128)} async-done(((f32[128,128]{0,1:T(8,128)}), f32[4096,128]{0,1:T(8,128)}) %all-gather.13.cloned.1.call-update) | async-done | bytes 2097168 | tf_op jit(solution)/shard_map/all_gather | solution.py:9
  189.7 1.9 copy.14
  191.6 56.4 %all-gather.15.cloned.1.call-done = f32[4096,128]{0,1:T(8,128)} async-done(((f32[128,128]{0,1:T(8,128)}), f32[4096,128]{0,1:T(8,128)}) %all-gather.15.cloned.1.call-update) | async-done | bytes 2097168 | tf_op jit(solution)/shard_map/all_gather | solution.py:9
  248.0 2.9 copy.15
  250.9 35.3 %while.31 = (s32[]{:T(128)}, f32[128,128]{1,0:T(8,128)S(1)}, s32[]{:T(128)}, f32[32,128,128]{2,1,0:T(8,128)S(1)}, f32[32,128,128]{2,1,0:T(8,128)}, /*index=5*/s32[]{:T(128)}, s32[]{:T(128)}, s32[]{:T(128)}, s32[]{:T(128)}) while((s32[]{:T(128)}, f32[128,128]{1,0:T(8,128)S(1)}, s32[]{:T(128)}, f32[32,128,128]{2,1,0:T(8,128)S(1)}, ...), condition=%wide.region_4.5_spmd.clone, body=%wide.region_3.4_spmd.clone.sunk | while | flops 25231368 | bytes 461469 | solution.py:22
  250.9 1.1 fusion.97
  252.1 1.1 fusion.97
  253.2 1.1 fusion.97
  254.3 1.1 fusion.97
  255.4 1.1 fusion.97
  258.7 1.1 fusion.97
  259.8 1.1 fusion.97
  260.9 1.1 fusion.97
  262.0 1.1 fusion.97
  265.3 1.1 fusion.97
  266.4 1.1 fusion.97
  267.5 1.1 fusion.97
  268.6 1.1 fusion.97
  271.9 1.1 fusion.97
  273.0 1.1 fusion.97
  274.1 1.1 fusion.97
  275.2 1.1 fusion.97
  278.5 1.1 fusion.97
  279.6 1.1 fusion.97
  280.7 1.1 fusion.97
  281.8 1.1 fusion.97
  285.1 1.1 fusion.97
  (137 shorter events, 33.0 us)
Async XLA Ops:
  7.2 25.0 %copy-start.1 = (f32[1,2,128,128]{3,2,1,0:T(8,128)S(1)}, f32[1,2,128,128]{3,2,1,0:T(8,128)}, u32[]{:S(2)}) copy-start(f32[1,2,128,128]{3,2,1,0:T(8,128)} %param.15) | copy-start | bytes 393220
  7.2 25.3 %copy-start = (f32[1,2,128,128]{3,2,1,0:T(8,128)S(1)}, f32[1,2,128,128]{3,2,1,0:T(8,128)}, u32[]{:S(2)}) copy-start(f32[1,2,128,128]{3,2,1,0:T(8,128)} %param.14) | copy-start | bytes 393220
  7.2 64.7 %all-gather.9.cloned.1.call-start = ((), (), s32[]{:S(2)}) async-start(), calls=%async_computation | async-start | bytes 2162688 | tf_op jit(solution)/shard_map/all_gather | solution.py:9
  12.3 118.1 %all-gather.11.cloned.1.call-start = ((), (), s32[]{:S(2)}) async-start(), calls=%async_computation.1 | async-start | bytes 2162688 | tf_op jit(solution)/shard_map/all_gather | solution.py:9
  13.1 6.3 %collective-permute-start = (f32[1,16,128]{2,1,0:T(8,128)S(1)}, f32[1,16,128]{2,1,0:T(8,128)S(1)}, u32[]{:S(2)}, u32[]{:S(2)}) collective-permute-start(f32[1,16,128]{2,1,0:T(8,128)S(1)} %get-tuple-element.303), channel_id=1, source_target_pairs={{0,8},{8,16},{16,24},{1,9},{9,17},{17,25},{2,10},{10,18},{18,26},{... | collective-permute-start | bytes 24584 | tf_op jit(solution)/shard_map/ppermute | solution.py:32
  18.0 5.5 %collective-permute-start.1 = (f32[1,16,128]{2,1,0:T(8,128)S(1)}, f32[1,16,128]{2,1,0:T(8,128)S(1)}, u32[]{:S(2)}, u32[]{:S(2)}) collective-permute-start(f32[1,16,128]{2,1,0:T(8,128)S(1)} %get-tuple-element.304), channel_id=1, source_target_pairs={{8,0},{16,8},{24,16},{9,1},{17,9},{25,17},{10,2},{18,10},{26,18},{... | collective-permute-start | bytes 24584 | tf_op jit(solution)/shard_map/ppermute | solution.py:33
  23.6 3.6 %collective-permute-start.2 = (f32[18,1,128]{2,1,0:T(1,128)S(1)}, f32[18,1,128]{2,1,0:T(1,128)S(1)}, u32[]{:S(2)}, u32[]{:S(2)}) collective-permute-start(f32[18,1,128]{2,1,0:T(1,128)S(1)} %get-tuple-element.299), channel_id=1, source_target_pairs={{0,1},{1,2},{2,3},{3,4},{4,5},{5,6},{6,7},{8,9},{9,10},{10,11},{11... | collective-permute-start | bytes 27656 | tf_op jit(solution)/shard_map/ppermute | solution.py:32
  24.9 4.8 %collective-permute-start.3 = (f32[18,1,128]{2,1,0:T(1,128)S(1)}, f32[18,1,128]{2,1,0:T(1,128)S(1)}, u32[]{:S(2)}, u32[]{:S(2)}) collective-permute-start(f32[18,1,128]{2,1,0:T(1,128)S(1)} %get-tuple-element.300), channel_id=1, source_target_pairs={{1,0},{2,1},{3,2},{4,3},{5,4},{6,5},{7,6},{9,8},{10,9},{11,10},{12... | collective-permute-start | bytes 27656 | tf_op jit(solution)/shard_map/ppermute | solution.py:33
  33.4 156.3 %all-gather.13.cloned.1.call-start = ((), (), s32[]{:S(2)}) async-start(), calls=%async_computation.2 | async-start | bytes 2162688 | tf_op jit(solution)/shard_map/all_gather | solution.py:9
  35.0 213.1 %all-gather.15.cloned.1.call-start = ((), (), s32[]{:S(2)}) async-start(), calls=%async_computation.3 | async-start | bytes 2162688 | tf_op jit(solution)/shard_map/all_gather | solution.py:9
  133.3 35.1 %copy-start.3 = (f32[128,128]{1,0:T(8,128)S(1)}, f32[128,128]{1,0:T(8,128)}, u32[]{:S(2)}) copy-start(f32[128,128]{1,0:T(8,128)} %convolution_negate_fusion.2) | copy-start | bytes 196612
  133.3 35.1 %copy-start.4 = (f32[128,128]{0,1:T(8,128)S(1)}, f32[128,128]{0,1:T(8,128)}, u32[]{:S(2)}) copy-start(f32[128,128]{0,1:T(8,128)} %convolution_bitcast_fusion.3) | copy-start | bytes 196612
  250.9 35.9 %copy-start.2 = (f32[16,16,128]{2,1,0:T(8,128)S(1)}, f32[16,16,128]{2,1,0:T(8,128)}, u32[]{:S(2)}) copy-start(f32[16,16,128]{2,1,0:T(8,128)} %param.10) | copy-start | bytes 393220
  286.8 0.9 copy-start.5
Sparse Core Ops, SparseCore 0:
  12.5 59.4 all-gather.8
  74.8 55.5 all-gather.10
  133.9 55.7 all-gather.12
  192.4 55.5 all-gather.14
where the time goes:
time: 298 us; the launch traced here: 294 us
  waiting for transfers between devices  175 us (59%)
  matrix products  79.1 us (27%)
  between operations  14.1 us (5%)
  local copies, waits for them, and re-layouts  11.8 us (4%)
  starting transfers between devices  8.95 us (3%)
  other arithmetic  3.08 us (1%)
    all_gather x4, waiting for transfers between devices, prefix(): everything = jax.tree.map(lambda part: lax.all_gather(part, axis), array)  169 us
    dot_general x75, matrix products, matmul(): jnp.dot(left, right, precision=lax.Precision.HIGHEST, preferred_element_t...  75.9 us
    unnamed x18, local copies, waits for them, and re-layouts  10.6 us
    ppermute x2, starting transfers between devices, extended(): before = lax.ppermute(last, axis, up)  6.21 us
  transfers between devices with their start and end apart: 8, of which 6 were waited for; matrix products, arithmetic and copies ran while one was open for 17% of the time, Pallas kernels for 0%

commit v1 on v0

v1 whole, which is shorter than its diff:
```python
import functools
import jax
import jax.numpy as jnp
from jax import lax
from jax.experimental import pallas as pl
from jax.experimental.pallas import tpu as pltpu
from jax.sharding import PartitionSpec as P

MESH = pl.DeviceIdType.MESH
F32 = jnp.float32
BF16 = jnp.bfloat16


def split(value):
    high = value.astype(BF16)
    return high, (value - high.astype(F32)).astype(BF16)


def product(left, right, transposed=False):
    dim = 0 if transposed else 1
    lh, ll = split(left)
    rh, rl = split(right)
    return lax.dot_general(
        jnp.concatenate([lh, ll, lh], axis=dim),
        jnp.concatenate([rh, rh, rl], axis=0),
        (((dim,), (0,)), ((), ())),
        preferred_element_type=F32,
    )


def pair(left, right):
    return jnp.concatenate([left, right], axis=1)


def kernel(n_front, n_lat, samples, reaction, weight_x, weight_y, inverses, couplings,
           white, grad, lap_x, lap_y, edges, halo_x, halo_y, maps, values, right_map, left_map,
           total, recv, halo_send, halo_recv, sends, recvs):
    front, lat = lax.axis_index("front"), lax.axis_index("lat")
    lat_rounds = n_lat.bit_length() - 1
    rounds = lat_rounds + n_front.bit_length() - 1
    tx, ty, count = samples.shape
    w = inverses.shape[-1]

    def bit_of(r):
        if r < lat_rounds:
            return lax.rem(lax.div(lat, 1 << r), 2)
        return lax.rem(lax.div(front, 1 << (r - lat_rounds)), 2)

    def partner(r):
        sign = 1 - 2 * bit_of(r)
        if r < lat_rounds:
            return (front, lat + sign * (1 << r))
        return (front + sign * (1 << (r - lat_rounds)), lat)

    neighbours = (
        (front < n_front - 1, (front + 1, lat)),
        (front > 0, (front - 1, lat)),
        (lat < n_lat - 1, (front, lat + 1)),
        (lat > 0, (front, lat - 1)),
    )

    barrier = pltpu.get_barrier_semaphore()
    for r in range(rounds):
        pl.semaphore_signal(barrier, inc=1, device_id=partner(r), device_id_type=MESH)
    for exists, target in neighbours:
        @pl.when(exists)
        def _(target=target):
            pl.semaphore_signal(barrier, inc=1, device_id=target, device_id_type=MESH)

    s = samples[...]
    edges[0] = s[:, ty - 1, :]
    edges[1] = s[:, 0, :]
    inv0, inv1 = inverses[0, 0], inverses[0, 1]
    t0 = -product(inv0, couplings[0, 0])
    t1 = -product(inv1, couplings[0, 1])
    maps[0] = t0
    maps[2] = t1

    peers = rounds
    for exists, _ in neighbours:
        peers = peers + exists.astype(jnp.int32)
    pl.semaphore_wait(barrier, peers)

    halos = []
    for i, (source, landing) in enumerate((
        (samples.at[tx - 1], halo_x.at[0]),
        (samples.at[0], halo_x.at[1]),
        (edges.at[0], halo_y.at[0]),
        (edges.at[1], halo_y.at[1]),
    )):
        halos.append(pltpu.make_async_remote_copy(
            src_ref=source, dst_ref=landing, send_sem=halo_send.at[i], recv_sem=halo_recv.at[i],
            device_id=neighbours[i][1], device_id_type=MESH))

        @pl.when(neighbours[i][0])
        def _(i=i):
            halos[i].start()

    full = product(t1, t0)
    maps[1] = full
    stack = maps[0:2].reshape(2 * w, w)
    total[0, 0] = full
    for i, landing in enumerate((halo_x.at[0], halo_x.at[1], halo_y.at[0], halo_y.at[1])):
        comes = neighbours[i ^ 1][0]

        @pl.when(comes)
        def _(i=i):
            halos[i].wait_recv()

        @pl.when(jnp.logical_not(comes))
        def _(landing=landing):
            landing[...] = jnp.zeros((landing.shape[0], count), F32)

    hx, hy = halo_x[...], halo_y[...]
    lx = 2.0 * s - jnp.concatenate([hx[0:1], s[:-1]], 0) - jnp.concatenate([s[1:], hx[1:2]], 0)
    ly = 2.0 * s - jnp.concatenate([hy[0][:, None, :], s[:, :-1]], 1) - jnp.concatenate([s[:, 1:], hy[1][:, None, :]], 1)
    lap_x[...] = lx
    lap_y[...] = ly
    resid = (reaction[...][:, :, None] * s + weight_x[...][:, :, None] * lx
             + weight_y[...][:, :, None] * ly).reshape(2 * w, count)
    y0 = product(inv0, resid[:w])
    y1 = product(inv1, resid[w:]) + product(t1, y0)
    values[0] = y0
    values[1] = y1
    total[0, 1] = y1
    adj = -product(stack, pair(stack, jnp.concatenate([y0, y1], 0)), True)
    total[0, 2] = adj[:, :w]
    total[0, 3] = adj[:, w:]

    def copy(r, part):
        if r == rounds - 1 and part == 0:
            window = pl.ds(1, 1)
        else:
            window = pl.ds(2 * part, 2)
        return pltpu.make_async_remote_copy(
            src_ref=total.at[r, window], dst_ref=recv.at[r, window],
            send_sem=sends.at[r, part], recv_sem=recvs.at[r, part],
            device_id=partner(r), device_id_type=MESH)

    def send(r, part):
        if r < rounds - 1:
            copy(r, part).start()
        else:
            @pl.when(bit_of(r) == part)
            def _():
                copy(r, part).start()

    send(0, 0)
    send(0, 1)
    eye = (lax.broadcasted_iota(jnp.int32, (w, w), 0) == lax.broadcasted_iota(jnp.int32, (w, w), 1)).astype(F32)
    zero = jnp.zeros((w, w), F32)
    left_map[0] = eye
    left_map[1] = zero
    right_map[0] = eye
    right_map[1] = zero
    right_map[2] = zero
    right_map[3] = zero

    def joined(earlier, later, store):
        start = earlier(0)
        ab = pair(start, earlier(1))
        new = product(later(0), ab)
        store(0, new[:, :w], new[:, w:] + later(1))
        mid = product(later(2), ab)
        mid = pair(mid[:, :w], mid[:, w:] + later(3))
        new = product(start, mid, True)
        store(1, earlier(2) + new[:, :w], earlier(3) + new[:, w:])

    for r in range(rounds - 1):
        copy(r, 0).wait_recv()
        copy(r, 1).wait_recv()

        def store_total(part, first, second, r=r):
            total[r + 1, 2 * part] = first
            total[r + 1, 2 * part + 1] = second
            send(r + 1, part)

        def store_right(part, first, second):
            right_map[2 * part] = first
            right_map[2 * part + 1] = second

        mine = lambda i, r=r: total[r, i]
        other = lambda i, r=r: recv[r, i]

        @pl.when(bit_of(r) == 0)
        def _():
            joined(mine, other, store_total)
            joined(lambda i: right_map[i], other, store_right)

        @pl.when(bit_of(r) == 1)
        def _():
            joined(other, mine, store_total)
            new = product(left_map[0], pair(other(0), other(1)))
            left_map[0] = new[:, :w]
            left_map[1] = new[:, w:] + left_map[1]

    r = rounds - 1

    @pl.when(bit_of(r) == 0)
    def _():
        copy(r, 1).wait_recv()
        middle = product(recv[r, 2], total[r, 1]) + recv[r, 3]
        right_map[3] = right_map[3] + product(right_map[0], middle, True)

    @pl.when(bit_of(r) == 1)
    def _():
        copy(r, 0).wait_recv()
        left_map[1] = product(left_map[0], recv[r, 1]) + left_map[1]

    y = values[...].reshape(2 * w, count) + product(maps[0:2].reshape(2 * w, w), left_map[1])
    c = product(right_map[2], y[w:]) + right_map[3]
    both = product(pair(inverses[0, 1], maps[2]), y[w:] - c, True)
    x0 = product(inverses[0, 0], y[:w] + both[w:], True)
    out = jnp.concatenate([x0, both[:w]], 0).reshape(tx, ty, count)
    white[...] = out
    grad[0] = jnp.sum(out * samples[...], axis=2) * (1.0 / count)
    grad[1] = jnp.sum(out * lap_x[...], axis=2) * (1.0 / count)
    grad[2] = jnp.sum(out * lap_y[...], axis=2) * (1.0 / count)

    for i in range(4):
        @pl.when(neighbours[i][0])
        def _(i=i):
            halos[i].wait_send()
    for r in range(rounds - 1):
        copy(r, 0).wait_send()
        copy(r, 1).wait_send()
    for part in range(2):
        @pl.when(bit_of(rounds - 1) == part)
        def _(part=part):
            copy(rounds - 1, part).wait_send()


def body(n_front, n_lat, samples, reaction, weight_x, weight_y, inverses, couplings):
    tx, ty, count = samples.shape
    w = inverses.shape[-1]
    rounds = n_lat.bit_length() + n_front.bit_length() - 2
    vmem = pl.BlockSpec(memory_space=pltpu.VMEM)
    return pl.pallas_call(
        functools.partial(kernel, n_front, n_lat),
        out_shape=(jax.ShapeDtypeStruct((tx, ty, count), F32), jax.ShapeDtypeStruct((3, tx, ty), F32)),
        in_specs=[vmem] * 6,
        out_specs=(vmem, vmem),
        scratch_shapes=[
            pltpu.VMEM((tx, ty, count), F32),
            pltpu.VMEM((tx, ty, count), F32),
            pltpu.VMEM((2, tx, count), F32),
            pltpu.VMEM((2, ty, count), F32),
            pltpu.VMEM((2, tx, count), F32),
            pltpu.VMEM((3, w, w), F32),
            pltpu.VMEM((2, w, count), F32),
            pltpu.VMEM((4, w, w), F32),
            pltpu.VMEM((2, w, w), F32),
            pltpu.VMEM((rounds, 4, w, w), F32),
            pltpu.VMEM((rounds, 4, w, w), F32),
            pltpu.SemaphoreType.DMA((4,)),
            pltpu.SemaphoreType.DMA((4,)),
            pltpu.SemaphoreType.DMA((rounds, 2)),
            pltpu.SemaphoreType.DMA((rounds, 2)),
        ],
        compiler_params=pltpu.CompilerParams(
            collective_id=0, has_side_effects=True, vmem_limit_bytes=48 * 1024 * 1024),
    )(samples, reaction, weight_x, weight_y, inverses, couplings)


def solution(mesh):
    placed = (
        P("front", "lat", None),
        P("front", "lat"),
        P("front", "lat"),
        P("front", "lat"),
        P("front", "lat", None, None),
        P("front", "lat", None, None),
    )
    return jax.shard_map(
        functools.partial(body, mesh.shape["front"], mesh.shape["lat"]),
        mesh=mesh,
        in_specs=placed,
        out_specs=(P("front", "lat", None), P(None, "front", "lat")),
        check_vma=False,
    )
```

time: 298 us -> 48.8 us (0.16); the launches traced: 294 us -> 48.4 us
  waiting for transfers between devices: 175 us -> 0 us
  matrix products: 79.1 us -> 0 us
  Pallas kernels: 0 us -> 41.7 us
  between operations: 14.1 us -> 0.65 us
  starting transfers between devices: 8.95 us -> 0 us
  local copies, waits for them, and re-layouts: 11.8 us -> 6.06 us
  other arithmetic: 3.08 us -> 0 us
    all_gather x4 -> x0, waiting for transfers between devices: 169 us -> none  [prefix(): everything = jax.tree.map(lambda part: lax.all_gather(part, axis), array)]
    dot_general x83 -> x0, matrix products: 79.1 us -> none  [the longest x75 75.9 us: matmul(): jnp.dot(left, right, precision=lax.Precision.HIGHEST, preferred_element_t...]
    pallas_call x0 -> x1, Pallas kernels: none -> 41.7 us  [body(): pl.pallas_call(functools.partial(kernel, n_front, n_lat), out_shape=(jax....]
    ppermute x4 -> x0, starting transfers between devices: 8.79 us -> none  [the longest x2 6.21 us: extended(): before = lax.ppermute(last, axis, up)]
    ppermute x4 -> x0, waiting for transfers between devices: 5.78 us -> none  [the longest x2 5.73 us: extended(): after = lax.ppermute(initial, axis, down)]
    unnamed x18 -> x14, local copies, waits for them, and re-layouts: 10.6 us -> 6.06 us
  transfers between devices with their start and end apart: 8 -> 0, of which waited for: 6 -> 0; matrix products, arithmetic and copies ran while one was open for 17% -> 0% of each run, Pallas kernels for 0% -> 0%
where the time goes in v1:
time: 48.8 us; the launch traced here: 48.4 us
  Pallas kernels  41.7 us (85%)
  local copies, waits for them, and re-layouts  6.06 us (12%)
  between operations  0.65 us (1%)
    pallas_call x1, Pallas kernels, body(): pl.pallas_call(functools.partial(kernel, n_front, n_lat), out_shape=(jax....  41.7 us
    unnamed x14, local copies, waits for them, and re-layouts  6.06 us

profile of v1, /device:TPU:0, one launch (start us, length us, event | category | flops | bytes accessed | tf_op | source)
XLA Modules:
  0.0 48.4 jit_solution(10676791459151681026)
XLA Ops:
  0.6 0.0 copy-start
  0.6 0.9 %copy-done = f32[16,16,128]{2,1,0:T(8,128)S(1)} copy-done((f32[16,16,128]{2,1,0:T(8,128)S(1)}, f32[16,16,128]{2,1,0:T(8,128)}, u32[]{:S(2)}) %copy-start) | copy-done | bytes 131096
  1.5 0.0 copy-start.1
  1.5 0.9 %copy-done.1 = f32[1,2,128,128]{3,2,1,0:T(8,128)S(1)} copy-done((f32[1,2,128,128]{3,2,1,0:T(8,128)S(1)}, f32[1,2,128,128]{3,2,1,0:T(8,128)}, u32[]{:S(2)}) %copy-start.1) | copy-done | bytes 131096
  2.4 0.0 copy-start.2
  2.4 0.9 %copy-done.2 = f32[1,2,128,128]{3,2,1,0:T(8,128)S(1)} copy-done((f32[1,2,128,128]{3,2,1,0:T(8,128)S(1)}, f32[1,2,128,128]{3,2,1,0:T(8,128)}, u32[]{:S(2)}) %copy-start.2) | copy-done | bytes 131096
  3.3 0.0 copy-start.3
  3.3 0.7 %copy-done.3 = f32[16,16]{1,0:T(8,128)S(1)} copy-done((f32[16,16]{1,0:T(8,128)S(1)}, f32[16,16]{1,0:T(8,128)}, u32[]{:S(2)}) %copy-start.3) | copy-done | bytes 1048
  4.0 0.0 copy-start.4
  4.0 0.7 %copy-done.4 = f32[16,16]{1,0:T(8,128)S(1)} copy-done((f32[16,16]{1,0:T(8,128)S(1)}, f32[16,16]{1,0:T(8,128)}, u32[]{:S(2)}) %copy-start.4) | copy-done | bytes 1048
  4.7 0.0 copy-start.5
  4.7 0.7 %copy-done.5 = f32[16,16]{1,0:T(8,128)S(1)} copy-done((f32[16,16]{1,0:T(8,128)S(1)}, f32[16,16]{1,0:T(8,128)}, u32[]{:S(2)}) %copy-start.5) | copy-done | bytes 1048
  5.4 41.7 %shard_map.77 = (f32[16,16,128]{2,1,0:T(8,128)S(1)}, f32[3,16,16]{2,1,0:T(8,128)S(1)}) custom-call(f32[16,16,128]{2,1,0:T(8,128)S(1)} %copy-done, f32[16,16]{1,0:T(8,128)S(1)} %copy-done.3, f32[16,16]{1,0:T(8,128)S(1)} %copy-done.4, f32[16,16]{1,0:T(8,128)S(1)} %copy-done.5, f32[1,2,128,128]{3,2,1,0:T(8,128)S(1)} %copy-done.1, f32[1,2,128,128]{3,2,1,0:T(8,128)S(1)} %copy-done.2), custom_call_target="tpu_custom_call" | custom-call | tf_op jit(solution)/shard_map/pallas_call | solution.py:238
  47.2 0.7 %copy.10 = f32[16,16,128]{2,1,0:T(8,128)} copy(f32[16,16,128]{2,1,0:T(8,128)S(1)} %get-tuple-element.4) | data formatting | bytes 262144
  47.8 0.6 %copy.11 = f32[3,16,16]{2,1,0:T(8,128)} copy(f32[3,16,16]{2,1,0:T(8,128)S(1)} %get-tuple-element.5) | data formatting | bytes 6144
Async XLA Ops:
  0.6 0.9 %copy-start = (f32[16,16,128]{2,1,0:T(8,128)S(1)}, f32[16,16,128]{2,1,0:T(8,128)}, u32[]{:S(2)}) copy-start(f32[16,16,128]{2,1,0:T(8,128)} %samples.1) | copy-start | bytes 393220
  1.5 0.9 %copy-start.1 = (f32[1,2,128,128]{3,2,1,0:T(8,128)S(1)}, f32[1,2,128,128]{3,2,1,0:T(8,128)}, u32[]{:S(2)}) copy-start(f32[1,2,128,128]{3,2,1,0:T(8,128)} %inverses.1) | copy-start | bytes 393220
  2.4 0.9 %copy-start.2 = (f32[1,2,128,128]{3,2,1,0:T(8,128)S(1)}, f32[1,2,128,128]{3,2,1,0:T(8,128)}, u32[]{:S(2)}) copy-start(f32[1,2,128,128]{3,2,1,0:T(8,128)} %couplings.1) | copy-start | bytes 393220
  3.3 0.7 %copy-start.3 = (f32[16,16]{1,0:T(8,128)S(1)}, f32[16,16]{1,0:T(8,128)}, u32[]{:S(2)}) copy-start(f32[16,16]{1,0:T(8,128)} %reaction.1) | copy-start | bytes 3076
  4.0 0.7 %copy-start.4 = (f32[16,16]{1,0:T(8,128)S(1)}, f32[16,16]{1,0:T(8,128)}, u32[]{:S(2)}) copy-start(f32[16,16]{1,0:T(8,128)} %weight_x.1) | copy-start | bytes 3076
  4.7 0.7 %copy-start.5 = (f32[16,16]{1,0:T(8,128)S(1)}, f32[16,16]{1,0:T(8,128)}, u32[]{:S(2)}) copy-start(f32[16,16]{1,0:T(8,128)} %weight_y.1) | copy-start | bytes 3076

commit v2 on v1

--- a/solution.py
+++ b/solution.py
@@ -32,8 +32,8 @@
     return jnp.concatenate([left, right], axis=1)
 
 
-def kernel(n_front, n_lat, samples, reaction, weight_x, weight_y, inverses, couplings,
-           white, grad, lap_x, lap_y, edges, halo_x, halo_y, maps, values, right_map, left_map,
+def kernel(n_front, n_lat, samples_in, reaction_in, weight_x_in, weight_y_in, inverses_in, couplings_in,
+           white, grad, samples, reaction, weight_x, weight_y, inverses, couplings, loads, lap_x, lap_y, edges, halo_x, halo_y, maps, values, right_map, left_map,
            total, recv, halo_send, halo_recv, sends, recvs):
     front, lat = lax.axis_index("front"), lax.axis_index("lat")
     lat_rounds = n_lat.bit_length() - 1
@@ -59,6 +59,12 @@
         (lat > 0, (front, lat - 1)),
     )
 
+    inputs = [
+        pltpu.make_async_copy(source, here, loads.at[i]) for i, (source, here) in enumerate((
+            (samples_in, samples), (reaction_in, reaction), (weight_x_in, weight_x),
+            (weight_y_in, weight_y), (inverses_in, inverses), (couplings_in, couplings)))]
+    for i in (0, 4, 5, 1, 2, 3):
+        inputs[i].start()
     barrier = pltpu.get_barrier_semaphore()
     for r in range(rounds):
         pl.semaphore_signal(barrier, inc=1, device_id=partner(r), device_id_type=MESH)
@@ -67,9 +73,13 @@
         def _(target=target):
             pl.semaphore_signal(barrier, inc=1, device_id=target, device_id_type=MESH)
 
+    samples_copy, reaction_copy, weight_x_copy, weight_y_copy, inverses_copy, couplings_copy = inputs
+    samples_copy.wait()
     s = samples[...]
     edges[0] = s[:, ty - 1, :]
     edges[1] = s[:, 0, :]
+    inverses_copy.wait()
+    couplings_copy.wait()
     inv0, inv1 = inverses[0, 0], inverses[0, 1]
     t0 = -product(inv0, couplings[0, 0])
     t1 = -product(inv1, couplings[0, 1])
@@ -111,6 +121,9 @@
         def _(landing=landing):
             landing[...] = jnp.zeros((landing.shape[0], count), F32)
 
+    reaction_copy.wait()
+    weight_x_copy.wait()
+    weight_y_copy.wait()
     hx, hy = halo_x[...], halo_y[...]
     lx = 2.0 * s - jnp.concatenate([hx[0:1], s[:-1]], 0) - jnp.concatenate([s[1:], hx[1:2]], 0)
     ly = 2.0 * s - jnp.concatenate([hy[0][:, None, :], s[:, :-1]], 1) - jnp.concatenate([s[:, 1:], hy[1][:, None, :]], 1)
@@ -123,30 +136,54 @@
     values[0] = y0
     values[1] = y1
     total[0, 1] = y1
+    core = bit_of(0)
+
+    def swap(part):
+        window = pl.ds(2 * part, 2)
+        return pltpu.make_async_remote_copy(
+            src_ref=total.at[0, window], dst_ref=recv.at[0, window],
+            send_sem=sends.at[0, part], recv_sem=recvs.at[0, part],
+            device_id=partner(0), device_id_type=MESH)
+
+    def piece(ref, r, kind, which):
+        if kind == 0:
+            return ref.at[r, 1, pl.ds(which * (w // 2), w // 2)]
+        if kind == 1:
+            return ref.at[r, pl.ds(2 + which, 1)]
+        return ref.at[r, pl.ds(2 * which, 2)]
+
+    def direct(r, kind=2, which=core):
+        return pltpu.make_async_remote_copy(
+            src_ref=piece(total, r, kind, which), dst_ref=piece(recv, r, kind, which),
+            send_sem=sends.at[r, 0], recv_sem=recvs.at[r, which],
+            device_id=partner(r), device_id_type=MESH)
+
+    def relay(r, kind=2, which=core):
+        return pltpu.make_async_remote_copy(
+            src_ref=piece(recv, r, kind, which), dst_ref=piece(recv, r, kind, which),
+            send_sem=sends.at[r, 1], recv_sem=recvs.at[r, which],
+            device_id=partner(0), device_id_type=MESH)
+
+    def receive(r, kind=2):
+        direct(r, kind).wait_recv()
+        relay(r, kind).start()
+        relay(r, kind, 1 - core).wait_recv()
+
+    def send(r, part):
+        if r < rounds - 1:
+            @pl.when(core == part)
+            def _():
+                direct(r, which=part).start()
+        else:
+            @pl.when(bit_of(r) == part)
+            def _():
+                direct(r, part).start()
+
+    swap(0).start()
     adj = -product(stack, pair(stack, jnp.concatenate([y0, y1], 0)), True)
     total[0, 2] = adj[:, :w]
     total[0, 3] = adj[:, w:]
-
-    def copy(r, part):
-        if r == rounds - 1 and part == 0:
-            window = pl.ds(1, 1)
-        else:
-            window = pl.ds(2 * part, 2)
-        return pltpu.make_async_remote_copy(
-            src_ref=total.at[r, window], dst_ref=recv.at[r, window],
-            send_sem=sends.at[r, part], recv_sem=recvs.at[r, part],
-            device_id=partner(r), device_id_type=MESH)
-
-    def send(r, part):
-        if r < rounds - 1:
-            copy(r, part).start()
-        else:
-            @pl.when(bit_of(r) == part)
-            def _():
-                copy(r, part).start()
-
-    send(0, 0)
-    send(0, 1)
+    swap(1).start()
     eye = (lax.broadcasted_iota(jnp.int32, (w, w), 0) == lax.broadcasted_iota(jnp.int32, (w, w), 1)).astype(F32)
     zero = jnp.zeros((w, w), F32)
     left_map[0] = eye
@@ -159,16 +196,18 @@
     def joined(earlier, later, store):
         start = earlier(0)
         ab = pair(start, earlier(1))
-        new = product(later(0), ab)
-        store(0, new[:, :w], new[:, w:] + later(1))
-        mid = product(later(2), ab)
-        mid = pair(mid[:, :w], mid[:, w:] + later(3))
+        both = product(jnp.concatenate([later(0), later(2)], 0), ab)
+        store(0, both[:w, :w], both[:w, w:] + later(1))
+        mid = pair(both[w:, :w], both[w:, w:] + later(3))
         new = product(start, mid, True)
         store(1, earlier(2) + new[:, :w], earlier(3) + new[:, w:])
 
     for r in range(rounds - 1):
-        copy(r, 0).wait_recv()
-        copy(r, 1).wait_recv()
+        if r == 0:
+            swap(0).wait_recv()
+            swap(1).wait_recv()
+        else:
+            receive(r)
 
         def store_total(part, first, second, r=r):
             total[r + 1, 2 * part] = first
@@ -198,13 +237,13 @@
 
     @pl.when(bit_of(r) == 0)
     def _():
-        copy(r, 1).wait_recv()
+        receive(r, 1)
         middle = product(recv[r, 2], total[r, 1]) + recv[r, 3]
         right_map[3] = right_map[3] + product(right_map[0], middle, True)
 
     @pl.when(bit_of(r) == 1)
     def _():
-        copy(r, 0).wait_recv()
+        receive(r, 0)
         left_map[1] = product(left_map[0], recv[r, 1]) + left_map[1]
 
     y = values[...].reshape(2 * w, count) + product(maps[0:2].reshape(2 * w, w), left_map[1])
@@ -221,16 +260,20 @@
         @pl.when(neighbours[i][0])
         def _(i=i):
             halos[i].wait_send()
-    for r in range(rounds - 1):
-        copy(r, 0).wait_send()
-        copy(r, 1).wait_send()
+    swap(0).wait_send()
+    swap(1).wait_send()
+    for r in range(1, rounds - 1):
+        direct(r).wait_send()
+        relay(r).wait_send()
     for part in range(2):
         @pl.when(bit_of(rounds - 1) == part)
         def _(part=part):
-            copy(rounds - 1, part).wait_send()
-
-
-def body(n_front, n_lat, samples, reaction, weight_x, weight_y, inverses, couplings):
+            direct(rounds - 1, part).wait_send()
+            relay(rounds - 1, 1 - part).wait_send()
+
+
+def body(n_front, n_lat, *arrays):
+    samples, inverses = arrays[0], arrays[4]
     tx, ty, count = samples.shape
     w = inverses.shape[-1]
     rounds = n_lat.bit_length() + n_front.bit_length() - 2
@@ -238,9 +281,11 @@
     return pl.pallas_call(
         functools.partial(kernel, n_front, n_lat),
         out_shape=(jax.ShapeDtypeStruct((tx, ty, count), F32), jax.ShapeDtypeStruct((3, tx, ty), F32)),
-        in_specs=[vmem] * 6,
+        in_specs=[pl.BlockSpec(memory_space=pltpu.HBM)] * 6,
         out_specs=(vmem, vmem),
         scratch_shapes=[
+            *[pltpu.VMEM(a.shape, F32) for a in arrays],
+            pltpu.SemaphoreType.DMA((6,)),
             pltpu.VMEM((tx, ty, count), F32),
             pltpu.VMEM((tx, ty, count), F32),
             pltpu.VMEM((2, tx, count), F32),
@@ -258,8 +303,8 @@
             pltpu.SemaphoreType.DMA((rounds, 2)),
         ],
         compiler_params=pltpu.CompilerParams(
-            collective_id=0, has_side_effects=True, vmem_limit_bytes=48 * 1024 * 1024),
-    )(samples, reaction, weight_x, weight_y, inverses, couplings)
+            collective_id=0, has_side_effects=True, vmem_limit_bytes=64 * 1024 * 1024 - 128 * 1024),
+    )(*arrays)
 
 
 def solution(mesh):

time: 48.8 us -> 39.5 us (0.81)
  the two profiles are of different devices: /device:TPU:0 before, /device:TPU:3 now
where the time goes in v2:
time: 39.5 us; the launch traced here: 39.4 us
  Pallas kernels  36.5 us (92%)
  local copies, waits for them, and re-layouts  2.19 us (6%)
  between operations  0.65 us (2%)
    pallas_call x1, Pallas kernels, body(): pl.pallas_call(functools.partial(kernel, n_front, n_lat), out_shape=(jax....  36.5 us
    unnamed x4, local copies, waits for them, and re-layouts  2.19 us

profile of v2, /device:TPU:3, one launch (start us, length us, event | category | flops | bytes accessed | tf_op | source)
XLA Modules:
  0.0 39.4 jit_solution(8569941394040055567)
XLA Ops:
  0.6 36.5 %shard_map.77 = (f32[16,16,128]{2,1,0:T(8,128)}, f32[3,16,16]{2,1,0:T(8,128)}) custom-call(f32[16,16,128]{2,1,0:T(8,128)} %samples_in.1, f32[16,16]{1,0:T(8,128)} %reaction_in.1, f32[16,16]{1,0:T(8,128)} %weight_x_in.1, f32[16,16]{1,0:T(8,128)} %weight_y_in.1, f32[1,2,128,128]{3,2,1,0:T(8,128)} %inverses_in.1, f32[1,2,128,128]{3,2,1,0:T(8,128)} %couplings_in.1), custom_call_target="tpu_custom_call" | custom-call | tf_op jit(solution)/shard_map/pallas_call | solution.py:281
  37.2 0.0 copy-start
  37.2 1.6 %copy.10 = f32[16,16,128]{2,1,0:T(8,128)} copy(f32[16,16,128]{2,1,0:T(8,128)} %get-tuple-element.4) | data formatting | bytes 262144
  38.8 0.0 copy-done
  38.8 0.6 %copy.11 = f32[3,16,16]{2,1,0:T(8,128)} copy(f32[3,16,16]{2,1,0:T(8,128)S(1)} %copy-done) | data formatting | bytes 6144
Async XLA Ops:
  37.2 1.6 %copy-start = (f32[3,16,16]{2,1,0:T(8,128)S(1)}, f32[3,16,16]{2,1,0:T(8,128)}, u32[]{:S(2)}) copy-start(f32[3,16,16]{2,1,0:T(8,128)} %get-tuple-element.5) | copy-start | bytes 9220

commit v3 on v2

--- a/solution.py
+++ b/solution.py
@@ -152,32 +152,49 @@
             return ref.at[r, pl.ds(2 + which, 1)]
         return ref.at[r, pl.ds(2 * which, 2)]
 
-    def direct(r, kind=2, which=core):
+    def remote(source, landing, sent, arrived, target):
         return pltpu.make_async_remote_copy(
-            src_ref=piece(total, r, kind, which), dst_ref=piece(recv, r, kind, which),
-            send_sem=sends.at[r, 0], recv_sem=recvs.at[r, which],
-            device_id=partner(r), device_id_type=MESH)
-
-    def relay(r, kind=2, which=core):
-        return pltpu.make_async_remote_copy(
-            src_ref=piece(recv, r, kind, which), dst_ref=piece(recv, r, kind, which),
-            send_sem=sends.at[r, 1], recv_sem=recvs.at[r, which],
-            device_id=partner(0), device_id_type=MESH)
-
-    def receive(r, kind=2):
-        direct(r, kind).wait_recv()
-        relay(r, kind).start()
+            src_ref=source, dst_ref=landing, send_sem=sent, recv_sem=arrived,
+            device_id=target, device_id_type=MESH)
+
+    def direct(r, kind, which):
+        return remote(piece(total, r, kind, which), piece(recv, r, kind, which),
+                      sends.at[r, 0], recvs.at[r, which], partner(r))
+
+    def relay(r, kind, which):
+        return remote(piece(recv, r, kind, which), piece(recv, r, kind, which),
+                      sends.at[r, 2], recvs.at[r, which], partner(0))
+
+    def receive(r, kind):
+        direct(r, kind, core).wait_recv()
+        relay(r, kind, core).start()
         relay(r, kind, 1 - core).wait_recv()
+
+    def matrix(side, which, k):
+        return which + 2 * k if side == 0 else 2 * which + k
+
+    def give(r, side, k, which=core):
+        m = matrix(side, which, k)
+        return remote(total.at[r, m], recv.at[r, m], sends.at[r, k], recvs.at[r, m], partner(r))
+
+    def hand(r, side, k, which=core):
+        m = matrix(side, which, k)
+        return remote(recv.at[r, m], recv.at[r, m], sends.at[r, 2 + k], recvs.at[r, m], partner(0))
 
     def send(r, part):
         if r < rounds - 1:
-            @pl.when(core == part)
+            @pl.when(bit_of(r) == 0)
             def _():
-                direct(r, which=part).start()
+                give(r, 0, part).start()
+
+            @pl.when((bit_of(r) == 1) & (core == part))
+            def _():
+                give(r, 1, 0, part).start()
+                give(r, 1, 1, part).start()
         else:
             @pl.when(bit_of(r) == part)
             def _():
-                direct(r, part).start()
+                direct(r, part, core).start()
 
     swap(0).start()
     adj = -product(stack, pair(stack, jnp.concatenate([y0, y1], 0)), True)
@@ -193,22 +210,20 @@
     right_map[2] = zero
     right_map[3] = zero
 
-    def joined(earlier, later, store):
+    def joined(earlier, later, store, needs=(None, None, None)):
+        wait = lambda i: needs[i]() if needs[i] else None
         start = earlier(0)
         ab = pair(start, earlier(1))
         both = product(jnp.concatenate([later(0), later(2)], 0), ab)
+        wait(0)
         store(0, both[:w, :w], both[:w, w:] + later(1))
+        wait(1)
         mid = pair(both[w:, :w], both[w:, w:] + later(3))
         new = product(start, mid, True)
+        wait(2)
         store(1, earlier(2) + new[:, :w], earlier(3) + new[:, w:])
 
     for r in range(rounds - 1):
-        if r == 0:
-            swap(0).wait_recv()
-            swap(1).wait_recv()
-        else:
-            receive(r)
-
         def store_total(part, first, second, r=r):
             total[r + 1, 2 * part] = first
             total[r + 1, 2 * part + 1] = second
@@ -221,14 +236,38 @@
         mine = lambda i, r=r: total[r, i]
         other = lambda i, r=r: recv[r, i]
 
+        def arrive(side, k, r=r):
+            give(r, side, k).wait_recv()
+            hand(r, side, k).start()
+
+        def settle(side, k, r=r):
+            hand(r, side, k, 1 - core).wait_recv()
+
+        if r == 0:
+            swap(0).wait_recv()
+            swap(1).wait_recv()
+
         @pl.when(bit_of(r) == 0)
         def _():
-            joined(mine, other, store_total)
+            def rest():
+                arrive(1, 1)
+                settle(1, 1)
+
+            if r > 0:
+                arrive(1, 0)
+                settle(1, 0)
+            joined(mine, other, store_total, (rest if r > 0 else None, None, None))
             joined(lambda i: right_map[i], other, store_right)
 
         @pl.when(bit_of(r) == 1)
         def _():
-            joined(other, mine, store_total)
+            if r > 0:
+                arrive(0, 0)
+                settle(0, 0)
+                needs = (None, functools.partial(arrive, 0, 1), functools.partial(settle, 0, 1))
+            else:
+                needs = (None, None, None)
+            joined(other, mine, store_total, needs)
             new = product(left_map[0], pair(other(0), other(1)))
             left_map[0] = new[:, :w]
             left_map[1] = new[:, w:] + left_map[1]
@@ -263,13 +302,17 @@
     swap(0).wait_send()
     swap(1).wait_send()
     for r in range(1, rounds - 1):
-        direct(r).wait_send()
-        relay(r).wait_send()
+        for side in range(2):
+            @pl.when(bit_of(r) == side)
+            def _(r=r, side=side):
+                for k in range(2):
+                    give(r, side, k).wait_send()
+                    hand(r, 1 - side, k).wait_send()
     for part in range(2):
         @pl.when(bit_of(rounds - 1) == part)
         def _(part=part):
-            direct(rounds - 1, part).wait_send()
-            relay(rounds - 1, 1 - part).wait_send()
+            direct(rounds - 1, part, core).wait_send()
+            relay(rounds - 1, 1 - part, core).wait_send()
 
 
 def body(n_front, n_lat, *arrays):
@@ -280,7 +323,7 @@
     vmem = pl.BlockSpec(memory_space=pltpu.VMEM)
     return pl.pallas_call(
         functools.partial(kernel, n_front, n_lat),
-        out_shape=(jax.ShapeDtypeStruct((tx, ty, count), F32), jax.ShapeDtypeStruct((3, tx, ty), F32)),
+        out_shape=(pltpu.VMEM((tx, ty, count), F32), pltpu.VMEM((3, tx, ty), F32)),
         in_specs=[pl.BlockSpec(memory_space=pltpu.HBM)] * 6,
         out_specs=(vmem, vmem),
         scratch_shapes=[
@@ -299,12 +342,12 @@
             pltpu.VMEM((rounds, 4, w, w), F32),
             pltpu.SemaphoreType.DMA((4,)),
             pltpu.SemaphoreType.DMA((4,)),
-            pltpu.SemaphoreType.DMA((rounds, 2)),
-            pltpu.SemaphoreType.DMA((rounds, 2)),
+            pltpu.SemaphoreType.DMA((rounds, 4)),
+            pltpu.SemaphoreType.DMA((rounds, 4)),
         ],
         compiler_params=pltpu.CompilerParams(
-            collective_id=0, has_side_effects=True, vmem_limit_bytes=64 * 1024 * 1024 - 128 * 1024),
-    )(*arrays)
+            collective_id=0, has_side_effects=True, vmem_limit_bytes=48 * 1024 * 1024),
+    )(*[pltpu.with_memory_space_constraint(a, pltpu.HBM) for a in arrays])
 
 
 def solution(mesh):

time: 39.5 us -> 37.3 us (0.944)
  the two profiles are of different devices: /device:TPU:3 before, /device:TPU:0 now
where the time goes in v3:
time: 37.3 us; the launch traced here: 37.2 us
  Pallas kernels  35.3 us (95%)
  local copies, waits for them, and re-layouts  1.27 us (3%)
  between operations  0.64 us (2%)
    pallas_call x1, Pallas kernels, body(): pl.pallas_call(functools.partial(kernel, n_front, n_lat), out_shape=(pltp...  35.3 us
    unnamed x2, local copies, waits for them, and re-layouts  1.27 us

profile of v3, /device:TPU:0, one launch (start us, length us, event | category | flops | bytes accessed | tf_op | source)
XLA Modules:
  0.0 37.2 jit_solution(9140398261427905536)
XLA Ops:
  0.6 35.3 %shard_map.77 = (f32[16,16,128]{2,1,0:T(8,128)S(1)}, f32[3,16,16]{2,1,0:T(8,128)S(1)}) custom-call(f32[16,16,128]{2,1,0:T(8,128)} %samples_in.1, f32[16,16]{1,0:T(8,128)} %reaction_in.1, f32[16,16]{1,0:T(8,128)} %weight_x_in.1, f32[16,16]{1,0:T(8,128)} %weight_y_in.1, f32[1,2,128,128]{3,2,1,0:T(8,128)} %inverses_in.1, f32[1,2,128,128]{3,2,1,0:T(8,128)} %couplings_in.1), custom_call_target="tpu_custom_call" | custom-call | tf_op jit(solution)/shard_map/pallas_call | solution.py:324
  35.9 0.7 %copy.10 = f32[16,16,128]{2,1,0:T(8,128)} copy(f32[16,16,128]{2,1,0:T(8,128)S(1)} %get-tuple-element.2) | data formatting | bytes 262144
  36.6 0.6 %copy.11 = f32[3,16,16]{2,1,0:T(8,128)} copy(f32[3,16,16]{2,1,0:T(8,128)S(1)} %get-tuple-element.3) | data formatting | bytes 6144

commit v4 on v3

--- a/solution.py
+++ b/solution.py
@@ -33,7 +33,7 @@
 
 
 def kernel(n_front, n_lat, samples_in, reaction_in, weight_x_in, weight_y_in, inverses_in, couplings_in,
-           white, grad, samples, reaction, weight_x, weight_y, inverses, couplings, loads, lap_x, lap_y, edges, halo_x, halo_y, maps, values, right_map, left_map,
+           white, grad, samples, reaction, weight_x, weight_y, inverses, couplings, loads, lap_x, lap_y, edges, halo_x, halo_y, maps, tails, values, right_map, left_map,
            total, recv, halo_send, halo_recv, sends, recvs):
     front, lat = lax.axis_index("front"), lax.axis_index("lat")
     lat_rounds = n_lat.bit_length() - 1
@@ -84,7 +84,6 @@
     t0 = -product(inv0, couplings[0, 0])
     t1 = -product(inv1, couplings[0, 1])
     maps[0] = t0
-    maps[2] = t1
 
     peers = rounds
     for exists, _ in neighbours:
@@ -110,6 +109,10 @@
     maps[1] = full
     stack = maps[0:2].reshape(2 * w, w)
     total[0, 0] = full
+    tail = product(t1, inv0)
+    tails[0] = inv1
+    tails[1] = tail
+    total[0, 2] = -product(stack, stack, True)
     for i, landing in enumerate((halo_x.at[0], halo_x.at[1], halo_y.at[0], halo_y.at[1])):
         comes = neighbours[i ^ 1][0]
 
@@ -132,7 +135,7 @@
     resid = (reaction[...][:, :, None] * s + weight_x[...][:, :, None] * lx
              + weight_y[...][:, :, None] * ly).reshape(2 * w, count)
     y0 = product(inv0, resid[:w])
-    y1 = product(inv1, resid[w:]) + product(t1, y0)
+    y1 = product(pair(tail, inv1), resid)
     values[0] = y0
     values[1] = y1
     total[0, 1] = y1
@@ -197,19 +200,10 @@
                 direct(r, part, core).start()
 
     swap(0).start()
-    adj = -product(stack, pair(stack, jnp.concatenate([y0, y1], 0)), True)
-    total[0, 2] = adj[:, :w]
-    total[0, 3] = adj[:, w:]
+    total[0, 3] = -product(stack, jnp.concatenate([y0, y1], 0), True)
     swap(1).start()
     eye = (lax.broadcasted_iota(jnp.int32, (w, w), 0) == lax.broadcasted_iota(jnp.int32, (w, w), 1)).astype(F32)
     zero = jnp.zeros((w, w), F32)
-    left_map[0] = eye
-    left_map[1] = zero
-    right_map[0] = eye
-    right_map[1] = zero
-    right_map[2] = zero
-    right_map[3] = zero
-
     def joined(earlier, later, store, needs=(None, None, None)):
         wait = lambda i: needs[i]() if needs[i] else None
         start = earlier(0)
@@ -257,7 +251,12 @@
                 arrive(1, 0)
                 settle(1, 0)
             joined(mine, other, store_total, (rest if r > 0 else None, None, None))
-            joined(lambda i: right_map[i], other, store_right)
+            if r > 0:
+                joined(lambda i: right_map[i], other, store_right)
+            else:
+                right_map[...] = recv[0]
+                left_map[0] = eye
+                left_map[1] = zero
 
         @pl.when(bit_of(r) == 1)
         def _():
@@ -268,29 +267,46 @@
             else:
                 needs = (None, None, None)
             joined(other, mine, store_total, needs)
-            new = product(left_map[0], pair(other(0), other(1)))
-            left_map[0] = new[:, :w]
-            left_map[1] = new[:, w:] + left_map[1]
+            if r > 0:
+                new = product(left_map[0], pair(other(0), other(1)))
+                left_map[0] = new[:, :w]
+                left_map[1] = new[:, w:] + left_map[1]
+            else:
+                left_map[...] = recv[0, 0:2]
+                right_map[0] = eye
+                right_map[1] = zero
+                right_map[2] = zero
+                right_map[3] = zero
 
     r = rounds - 1
+    stack = maps[...].reshape(2 * w, w)
+    tail = pair(tails[0], tails[1])
+
+    def finish(y):
+        rest = y[w:] - product(right_map[2], y[w:]) - right_map[3]
+        x = product(tail, rest, True)
+        return x[:w], x[w:] + product(inverses[0, 0], y[:w], True)
+
+    def put(x1, x0):
+        white[...] = jnp.concatenate([x0, x1], 0).reshape(tx, ty, count)
 
     @pl.when(bit_of(r) == 0)
     def _():
+        x1, x0 = finish(values[...].reshape(2 * w, count) + product(stack, left_map[1]))
+        back = product(right_map[0], tail)
         receive(r, 1)
         middle = product(recv[r, 2], total[r, 1]) + recv[r, 3]
-        right_map[3] = right_map[3] + product(right_map[0], middle, True)
+        change = product(back, middle, True)
+        put(x1 - change[:w], x0 - change[w:])
 
     @pl.when(bit_of(r) == 1)
     def _():
+        new = product(stack, pair(left_map[0], left_map[1]))
+        base = values[...].reshape(2 * w, count) + new[:, w:]
         receive(r, 0)
-        left_map[1] = product(left_map[0], recv[r, 1]) + left_map[1]
-
-    y = values[...].reshape(2 * w, count) + product(maps[0:2].reshape(2 * w, w), left_map[1])
-    c = product(right_map[2], y[w:]) + right_map[3]
-    both = product(pair(inverses[0, 1], maps[2]), y[w:] - c, True)
-    x0 = product(inverses[0, 0], y[:w] + both[w:], True)
-    out = jnp.concatenate([x0, both[:w]], 0).reshape(tx, ty, count)
-    white[...] = out
+        put(*finish(base + product(new[:, :w], recv[r, 1])))
+
+    out = white[...]
     grad[0] = jnp.sum(out * samples[...], axis=2) * (1.0 / count)
     grad[1] = jnp.sum(out * lap_x[...], axis=2) * (1.0 / count)
     grad[2] = jnp.sum(out * lap_y[...], axis=2) * (1.0 / count)
@@ -334,7 +350,8 @@
             pltpu.VMEM((2, tx, count), F32),
             pltpu.VMEM((2, ty, count), F32),
             pltpu.VMEM((2, tx, count), F32),
-            pltpu.VMEM((3, w, w), F32),
+            pltpu.VMEM((2, w, w), F32),
+            pltpu.VMEM((2, w, w), F32),
             pltpu.VMEM((2, w, count), F32),
             pltpu.VMEM((4, w, w), F32),
             pltpu.VMEM((2, w, w), F32),

time: 37.3 us -> 36.5 us (0.979)
  Pallas kernels: 35.3 us -> 34.5 us
    pallas_call x1, Pallas kernels: 35.3 us -> 34.5 us  [body(): pl.pallas_call(functools.partial(kernel, n_front, n_lat), out_shape=(pltp...]
where the time goes in v4:
time: 36.5 us; the launch traced here: 36.4 us
  Pallas kernels  34.5 us (95%)
  local copies, waits for them, and re-layouts  1.27 us (3%)
  between operations  0.64 us (2%)
    pallas_call x1, Pallas kernels, body(): pl.pallas_call(functools.partial(kernel, n_front, n_lat), out_shape=(pltp...  34.5 us
    unnamed x2, local copies, waits for them, and re-layouts  1.27 us

profile of v4, /device:TPU:0, one launch (start us, length us, event | category | flops | bytes accessed | tf_op | source)
XLA Modules:
  0.0 36.4 jit_solution(10069597089100561558)
XLA Ops:
  0.6 34.5 %shard_map.77 = (f32[16,16,128]{2,1,0:T(8,128)S(1)}, f32[3,16,16]{2,1,0:T(8,128)S(1)}) custom-call(f32[16,16,128]{2,1,0:T(8,128)} %samples_in.1, f32[16,16]{1,0:T(8,128)} %reaction_in.1, f32[16,16]{1,0:T(8,128)} %weight_x_in.1, f32[16,16]{1,0:T(8,128)} %weight_y_in.1, f32[1,2,128,128]{3,2,1,0:T(8,128)} %inverses_in.1, f32[1,2,128,128]{3,2,1,0:T(8,128)} %couplings_in.1), custom_call_target="tpu_custom_call" | custom-call | tf_op jit(solution)/shard_map/pallas_call | solution.py:340
  35.1 0.7 %copy.10 = f32[16,16,128]{2,1,0:T(8,128)} copy(f32[16,16,128]{2,1,0:T(8,128)S(1)} %get-tuple-element.2) | data formatting | bytes 262144
  35.8 0.6 %copy.11 = f32[3,16,16]{2,1,0:T(8,128)} copy(f32[3,16,16]{2,1,0:T(8,128)S(1)} %get-tuple-element.3) | data formatting | bytes 6144

commit v5 on v4

--- a/solution.py
+++ b/solution.py
@@ -65,10 +65,14 @@
             (weight_y_in, weight_y), (inverses_in, inverses), (couplings_in, couplings)))]
     for i in (0, 4, 5, 1, 2, 3):
         inputs[i].start()
+    middle_step = 1 - 2 * bit_of(rounds - 1)
+    neighbours_all = neighbours + (
+        (bit_of(rounds - 2) != bit_of(rounds - 1),
+         (front + middle_step * (1 << (rounds - 2 - lat_rounds)), lat)),)
     barrier = pltpu.get_barrier_semaphore()
     for r in range(rounds):
         pl.semaphore_signal(barrier, inc=1, device_id=partner(r), device_id_type=MESH)
-    for exists, target in neighbours:
+    for exists, target in neighbours_all:
         @pl.when(exists)
         def _(target=target):
             pl.semaphore_signal(barrier, inc=1, device_id=target, device_id_type=MESH)
@@ -86,7 +90,7 @@
     maps[0] = t0
 
     peers = rounds
-    for exists, _ in neighbours:
+    for exists, _ in neighbours_all:
         peers = peers + exists.astype(jnp.int32)
     pl.semaphore_wait(barrier, peers)
 
@@ -184,8 +188,37 @@
         m = matrix(side, which, k)
         return remote(recv.at[r, m], recv.at[r, m], sends.at[r, 2 + k], recvs.at[r, m], partner(0))
 
+    first_bit, last_bit = bit_of(rounds - 2), bit_of(rounds - 1)
+
+    def quarter(p):
+        return (first_bit == p % 2) & (last_bit == p // 2)
+
+    def near(kind):
+        r = rounds - 1
+        step = (1 - 2 * kind) * (1 << (rounds - 2 - lat_rounds))
+        return remote(piece(total, r, kind, core), piece(recv, r, kind, core),
+                      sends.at[r, 1], recvs.at[r, core], (front + step, lat))
+
     def send(r, part):
-        if r < rounds - 1:
+        if r == rounds - 2:
+            if part == 0:
+                @pl.when(quarter(0))
+                def _():
+                    direct(r, 0, core).start()
+
+                @pl.when(quarter(2))
+                def _():
+                    give(r, 0, 0).start()
+            else:
+                @pl.when(quarter(3))
+                def _():
+                    direct(r, 1, core).start()
+
+            @pl.when(quarter(1) & (core == part))
+            def _():
+                give(r, 1, 0, part).start()
+                give(r, 1, 1, part).start()
+        else:
             @pl.when(bit_of(r) == 0)
             def _():
                 give(r, 0, part).start()
@@ -194,10 +227,6 @@
             def _():
                 give(r, 1, 0, part).start()
                 give(r, 1, 1, part).start()
-        else:
-            @pl.when(bit_of(r) == part)
-            def _():
-                direct(r, part, core).start()
 
     swap(0).start()
     total[0, 3] = -product(stack, jnp.concatenate([y0, y1], 0), True)
@@ -217,15 +246,15 @@
         wait(2)
         store(1, earlier(2) + new[:, :w], earlier(3) + new[:, w:])
 
-    for r in range(rounds - 1):
+    def store_right(part, first, second):
+        right_map[2 * part] = first
+        right_map[2 * part + 1] = second
+
+    for r in range(rounds - 2):
         def store_total(part, first, second, r=r):
             total[r + 1, 2 * part] = first
             total[r + 1, 2 * part + 1] = second
             send(r + 1, part)
-
-        def store_right(part, first, second):
-            right_map[2 * part] = first
-            right_map[2 * part + 1] = second
 
         mine = lambda i, r=r: total[r, i]
         other = lambda i, r=r: recv[r, i]
@@ -278,7 +307,52 @@
                 right_map[2] = zero
                 right_map[3] = zero
 
-    r = rounds - 1
+    r = rounds - 2
+
+    def quarter_arrive(side, k):
+        give(r, side, k).wait_recv()
+        hand(r, side, k).start()
+        hand(r, side, k, 1 - core).wait_recv()
+
+    @pl.when(quarter(0))
+    def _():
+        quarter_arrive(1, 0)
+        quarter_arrive(1, 1)
+        total[r + 1, 1] = product(recv[r, 0], total[r, 1]) + recv[r, 1]
+        joined(lambda i: right_map[i], lambda i: recv[r, i], store_right)
+
+    @pl.when(quarter(1))
+    def _():
+        receive(r, 0)
+        total[r + 1, 1] = product(total[r, 0], recv[r, 1]) + total[r, 1]
+        direct(r + 1, 0, core).start()
+        near(0).start()
+        left_map[1] = product(left_map[0], recv[r, 1]) + left_map[1]
+
+    def adjoint(a, b):
+        mid = product(recv[r, 2], pair(a, b))
+        return product(a, pair(mid[:, :w], mid[:, w:] + recv[r, 3]), True)
+
+    @pl.when(quarter(2))
+    def _():
+        receive(r, 1)
+        new = adjoint(total[r, 0], total[r, 1])
+        total[r + 1, 2] = total[r, 2] + new[:, :w]
+        total[r + 1, 3] = total[r, 3] + new[:, w:]
+        direct(r + 1, 1, core).start()
+        near(1).start()
+        new = adjoint(right_map[0], right_map[1])
+        right_map[2] = right_map[2] + new[:, :w]
+        right_map[3] = right_map[3] + new[:, w:]
+
+    @pl.when(quarter(3))
+    def _():
+        quarter_arrive(0, 0)
+        new = product(left_map[0], pair(recv[r, 0], recv[r, 1]))
+        left_map[0] = new[:, :w]
+        left_map[1] = new[:, w:] + left_map[1]
+
+    z = rounds - 1
     stack = maps[...].reshape(2 * w, w)
     tail = pair(tails[0], tails[1])
 
@@ -290,21 +364,21 @@
     def put(x1, x0):
         white[...] = jnp.concatenate([x0, x1], 0).reshape(tx, ty, count)
 
-    @pl.when(bit_of(r) == 0)
+    @pl.when(last_bit == 0)
     def _():
         x1, x0 = finish(values[...].reshape(2 * w, count) + product(stack, left_map[1]))
         back = product(right_map[0], tail)
-        receive(r, 1)
-        middle = product(recv[r, 2], total[r, 1]) + recv[r, 3]
+        receive(z, 1)
+        middle = product(recv[z, 2], total[z, 1]) + recv[z, 3]
         change = product(back, middle, True)
         put(x1 - change[:w], x0 - change[w:])
 
-    @pl.when(bit_of(r) == 1)
+    @pl.when(last_bit == 1)
     def _():
         new = product(stack, pair(left_map[0], left_map[1]))
         base = values[...].reshape(2 * w, count) + new[:, w:]
-        receive(r, 0)
-        put(*finish(base + product(new[:, :w], recv[r, 1])))
+        receive(z, 0)
+        put(*finish(base + product(new[:, :w], recv[z, 1])))
 
     out = white[...]
     grad[0] = jnp.sum(out * samples[...], axis=2) * (1.0 / count)
@@ -317,18 +391,24 @@
             halos[i].wait_send()
     swap(0).wait_send()
     swap(1).wait_send()
-    for r in range(1, rounds - 1):
+    for r in range(1, rounds - 2):
         for side in range(2):
             @pl.when(bit_of(r) == side)
             def _(r=r, side=side):
                 for k in range(2):
                     give(r, side, k).wait_send()
                     hand(r, 1 - side, k).wait_send()
-    for part in range(2):
-        @pl.when(bit_of(rounds - 1) == part)
-        def _(part=part):
-            direct(rounds - 1, part, core).wait_send()
-            relay(rounds - 1, 1 - part, core).wait_send()
+    r, z = rounds - 2, rounds - 1
+    for p, started in enumerate((
+        (direct(r, 0, core), hand(r, 1, 0), hand(r, 1, 1)),
+        (give(r, 1, 0), give(r, 1, 1), relay(r, 0, core), direct(z, 0, core), near(0)),
+        (give(r, 0, 0), relay(r, 1, core), direct(z, 1, core), near(1)),
+        (direct(r, 1, core), hand(r, 0, 0)),
+    )):
+        @pl.when(quarter(p))
+        def _(p=p, started=started):
+            for one in started + (relay(z, 1 - p // 2, core),):
+                one.wait_send()
 
 
 def body(n_front, n_lat, *arrays):

time: 36.5 us -> 34.2 us (0.937); the launches traced: 36.4 us -> 33.6 us
  Pallas kernels: 34.5 us -> 31.7 us
    pallas_call x1, Pallas kernels: 34.5 us -> 31.7 us  [body(): pl.pallas_call(functools.partial(kernel, n_front, n_lat), out_shape=(pltp...]
where the time goes in v5:
time: 34.2 us; the launch traced here: 33.6 us
  Pallas kernels  31.7 us (93%)
  local copies, waits for them, and re-layouts  1.27 us (4%)
  between operations  0.64 us (2%)
    pallas_call x1, Pallas kernels, body(): pl.pallas_call(functools.partial(kernel, n_front, n_lat), out_shape=(pltp...  31.7 us
    unnamed x2, local copies, waits for them, and re-layouts  1.27 us

profile of v5, /device:TPU:0, one launch (start us, length us, event | category | flops | bytes accessed | tf_op | source)
XLA Modules:
  0.0 33.6 jit_solution(10884068927629687599)
XLA Ops:
  0.6 31.7 %shard_map.77 = (f32[16,16,128]{2,1,0:T(8,128)S(1)}, f32[3,16,16]{2,1,0:T(8,128)S(1)}) custom-call(f32[16,16,128]{2,1,0:T(8,128)} %samples_in.1, f32[16,16]{1,0:T(8,128)} %reaction_in.1, f32[16,16]{1,0:T(8,128)} %weight_x_in.1, f32[16,16]{1,0:T(8,128)} %weight_y_in.1, f32[1,2,128,128]{3,2,1,0:T(8,128)} %inverses_in.1, f32[1,2,128,128]{3,2,1,0:T(8,128)} %couplings_in.1), custom_call_target="tpu_custom_call" | custom-call | tf_op jit(solution)/shard_map/pallas_call | solution.py:420
  32.3 0.7 %copy.10 = f32[16,16,128]{2,1,0:T(8,128)} copy(f32[16,16,128]{2,1,0:T(8,128)S(1)} %get-tuple-element.2) | data formatting | bytes 262144
  33.0 0.6 %copy.11 = f32[3,16,16]{2,1,0:T(8,128)} copy(f32[3,16,16]{2,1,0:T(8,128)S(1)} %get-tuple-element.3) | data formatting | bytes 6144

commit v6 on v5

--- a/solution.py
+++ b/solution.py
@@ -109,14 +109,134 @@
         def _(i=i):
             halos[i].start()
 
+    core = bit_of(0)
+
+    def swap(m):
+        return pltpu.make_async_remote_copy(
+            src_ref=total.at[0, m], dst_ref=recv.at[0, m],
+            send_sem=sends.at[0, m], recv_sem=recvs.at[0, m],
+            device_id=partner(0), device_id_type=MESH)
+
+    def piece(ref, r, kind, which):
+        if kind == 0:
+            return ref.at[r, 1, pl.ds(which * (w // 2), w // 2)]
+        if kind == 1:
+            return ref.at[r, pl.ds(2 + which, 1)]
+        return ref.at[r, pl.ds(2 * which, 2)]
+
+    def remote(source, landing, sent, arrived, target):
+        return pltpu.make_async_remote_copy(
+            src_ref=source, dst_ref=landing, send_sem=sent, recv_sem=arrived,
+            device_id=target, device_id_type=MESH)
+
+    def direct(r, kind, which):
+        return remote(piece(total, r, kind, which), piece(recv, r, kind, which),
+                      sends.at[r, 0], recvs.at[r, which], partner(r))
+
+    def relay(r, kind, which):
+        return remote(piece(recv, r, kind, which), piece(recv, r, kind, which),
+                      sends.at[r, 2], recvs.at[r, which], partner(0))
+
+    def receive(r, kind):
+        direct(r, kind, core).wait_recv()
+        relay(r, kind, core).start()
+        relay(r, kind, 1 - core).wait_recv()
+
+    def matrix(side, which, k):
+        return which + 2 * k if side == 0 else 2 * which + k
+
+    def give(r, side, k, which=core):
+        m = matrix(side, which, k)
+        return remote(total.at[r, m], recv.at[r, m], sends.at[r, k], recvs.at[r, m], partner(r))
+
+    def hand(r, side, k, which=core):
+        m = matrix(side, which, k)
+        return remote(recv.at[r, m], recv.at[r, m], sends.at[r, 2 + k], recvs.at[r, m], partner(0))
+
+    first_bit, last_bit = bit_of(rounds - 2), bit_of(rounds - 1)
+
+    def quarter(p):
+        return (first_bit == p % 2) & (last_bit == p // 2)
+
+    def near(kind):
+        r = rounds - 1
+        step = (1 - 2 * kind) * (1 << (rounds - 2 - lat_rounds))
+        return remote(piece(total, r, kind, core), piece(recv, r, kind, core),
+                      sends.at[r, 1], recvs.at[r, core], (front + step, lat))
+
+    def send(r, part):
+        if r == rounds - 2:
+            if part == 0:
+                @pl.when(quarter(0))
+                def _():
+                    direct(r, 0, core).start()
+
+                @pl.when(quarter(2))
+                def _():
+                    give(r, 0, 0).start()
+            else:
+                @pl.when(quarter(3))
+                def _():
+                    direct(r, 1, core).start()
+
+            @pl.when(quarter(1) & (core == part))
+            def _():
+                give(r, 1, 0, part).start()
+                give(r, 1, 1, part).start()
+        else:
+            @pl.when(bit_of(r) == 0)
+            def _():
+                give(r, 0, part).start()
+
+            @pl.when((bit_of(r) == 1) & (core == part))
+            def _():
+                give(r, 1, 0, part).start()
+                give(r, 1, 1, part).start()
+
     full = product(t1, t0)
     maps[1] = full
+    total[0, 0] = full
+    swap(0).start()
     stack = maps[0:2].reshape(2 * w, w)
-    total[0, 0] = full
+    total[0, 2] = -product(stack, stack, True)
+    swap(2).start()
     tail = product(t1, inv0)
     tails[0] = inv1
     tails[1] = tail
-    total[0, 2] = -product(stack, stack, True)
+
+    def first_matrices(earlier, later):
+        start = earlier[0, 0]
+        both = product(jnp.concatenate([later[0, 0], later[0, 2]], 0), start)
+        total[1, 0] = both[:w]
+        total[1, 2] = earlier[0, 2] + product(start, both[w:], True)
+
+    def first_vectors(earlier, later):
+        both = product(jnp.concatenate([later[0, 0], later[0, 2]], 0), earlier[0, 1])
+        total[1, 1] = both[:w] + later[0, 1]
+
+        @pl.when(core == 0)
+        def _():
+            give(1, 1, 1, 0).start()
+
+        total[1, 3] = earlier[0, 3] + product(earlier[0, 0], both[w:] + later[0, 3], True)
+
+        @pl.when(core == 1)
+        def _():
+            give(1, 1, 1, 1).start()
+
+    def first(step):
+        @pl.when(core == 0)
+        def _():
+            step(total, recv)
+
+        @pl.when(core == 1)
+        def _():
+            step(recv, total)
+
+    swap(0).wait_recv()
+    swap(2).wait_recv()
+    first(first_matrices)
+    give(1, 1, 0).start()
     for i, landing in enumerate((halo_x.at[0], halo_x.at[1], halo_y.at[0], halo_y.at[1])):
         comes = neighbours[i ^ 1][0]
 
@@ -143,96 +263,29 @@
     values[0] = y0
     values[1] = y1
     total[0, 1] = y1
-    core = bit_of(0)
-
-    def swap(part):
-        window = pl.ds(2 * part, 2)
-        return pltpu.make_async_remote_copy(
-            src_ref=total.at[0, window], dst_ref=recv.at[0, window],
-            send_sem=sends.at[0, part], recv_sem=recvs.at[0, part],
-            device_id=partner(0), device_id_type=MESH)
-
-    def piece(ref, r, kind, which):
-        if kind == 0:
-            return ref.at[r, 1, pl.ds(which * (w // 2), w // 2)]
-        if kind == 1:
-            return ref.at[r, pl.ds(2 + which, 1)]
-        return ref.at[r, pl.ds(2 * which, 2)]
-
-    def remote(source, landing, sent, arrived, target):
-        return pltpu.make_async_remote_copy(
-            src_ref=source, dst_ref=landing, send_sem=sent, recv_sem=arrived,
-            device_id=target, device_id_type=MESH)
-
-    def direct(r, kind, which):
-        return remote(piece(total, r, kind, which), piece(recv, r, kind, which),
-                      sends.at[r, 0], recvs.at[r, which], partner(r))
-
-    def relay(r, kind, which):
-        return remote(piece(recv, r, kind, which), piece(recv, r, kind, which),
-                      sends.at[r, 2], recvs.at[r, which], partner(0))
-
-    def receive(r, kind):
-        direct(r, kind, core).wait_recv()
-        relay(r, kind, core).start()
-        relay(r, kind, 1 - core).wait_recv()
-
-    def matrix(side, which, k):
-        return which + 2 * k if side == 0 else 2 * which + k
-
-    def give(r, side, k, which=core):
-        m = matrix(side, which, k)
-        return remote(total.at[r, m], recv.at[r, m], sends.at[r, k], recvs.at[r, m], partner(r))
-
-    def hand(r, side, k, which=core):
-        m = matrix(side, which, k)
-        return remote(recv.at[r, m], recv.at[r, m], sends.at[r, 2 + k], recvs.at[r, m], partner(0))
-
-    first_bit, last_bit = bit_of(rounds - 2), bit_of(rounds - 1)
-
-    def quarter(p):
-        return (first_bit == p % 2) & (last_bit == p // 2)
-
-    def near(kind):
-        r = rounds - 1
-        step = (1 - 2 * kind) * (1 << (rounds - 2 - lat_rounds))
-        return remote(piece(total, r, kind, core), piece(recv, r, kind, core),
-                      sends.at[r, 1], recvs.at[r, core], (front + step, lat))
-
-    def send(r, part):
-        if r == rounds - 2:
-            if part == 0:
-                @pl.when(quarter(0))
-                def _():
-                    direct(r, 0, core).start()
-
-                @pl.when(quarter(2))
-                def _():
-                    give(r, 0, 0).start()
-            else:
-                @pl.when(quarter(3))
-                def _():
-                    direct(r, 1, core).start()
-
-            @pl.when(quarter(1) & (core == part))
-            def _():
-                give(r, 1, 0, part).start()
-                give(r, 1, 1, part).start()
-        else:
-            @pl.when(bit_of(r) == 0)
-            def _():
-                give(r, 0, part).start()
-
-            @pl.when((bit_of(r) == 1) & (core == part))
-            def _():
-                give(r, 1, 0, part).start()
-                give(r, 1, 1, part).start()
-
-    swap(0).start()
+    swap(1).start()
     total[0, 3] = -product(stack, jnp.concatenate([y0, y1], 0), True)
-    swap(1).start()
+    swap(3).start()
+    swap(1).wait_recv()
+    swap(3).wait_recv()
+    first(first_vectors)
     eye = (lax.broadcasted_iota(jnp.int32, (w, w), 0) == lax.broadcasted_iota(jnp.int32, (w, w), 1)).astype(F32)
     zero = jnp.zeros((w, w), F32)
+
+    @pl.when(core == 0)
+    def _():
+        right_map[...] = recv[0]
+        left_map[0] = eye
+        left_map[1] = zero
+
+    @pl.when(core == 1)
+    def _():
+        left_map[...] = recv[0, 0:2]
+        right_map[0] = eye
+        right_map[1] = zero
+        right_map[2] = zero
+        right_map[3] = zero
+
     def joined(earlier, later, store, needs=(None, None, None)):
         wait = lambda i: needs[i]() if needs[i] else None
         start = earlier(0)
@@ -250,7 +303,7 @@
         right_map[2 * part] = first
         right_map[2 * part + 1] = second
 
-    for r in range(rounds - 2):
+    for r in range(1, rounds - 2):
         def store_total(part, first, second, r=r):
             total[r + 1, 2 * part] = first
             total[r + 1, 2 * part + 1] = second
@@ -265,10 +318,6 @@
 
         def settle(side, k, r=r):
             hand(r, side, k, 1 - core).wait_recv()
-
-        if r == 0:
-            swap(0).wait_recv()
-            swap(1).wait_recv()
 
         @pl.when(bit_of(r) == 0)
         def _():
@@ -276,36 +325,26 @@
                 arrive(1, 1)
                 settle(1, 1)
 
-            if r > 0:
-                arrive(1, 0)
-                settle(1, 0)
-            joined(mine, other, store_total, (rest if r > 0 else None, None, None))
-            if r > 0:
-                joined(lambda i: right_map[i], other, store_right)
-            else:
-                right_map[...] = recv[0]
-                left_map[0] = eye
-                left_map[1] = zero
+            arrive(1, 0)
+            settle(1, 0)
+            joined(mine, other, store_total, (rest, None, None))
+            joined(lambda i: right_map[i], other, store_right)
 
         @pl.when(bit_of(r) == 1)
         def _():
-            if r > 0:
+            if r == 1:
+                for k in range(2):
+                    arrive(1, k)
+                    settle(1, k)
+                joined(other, mine, store_total)
+            else:
                 arrive(0, 0)
                 settle(0, 0)
-                needs = (None, functools.partial(arrive, 0, 1), functools.partial(settle, 0, 1))
-            else:
-                needs = (None, None, None)
-            joined(other, mine, store_total, needs)
-            if r > 0:
-                new = product(left_map[0], pair(other(0), other(1)))
-                left_map[0] = new[:, :w]
-                left_map[1] = new[:, w:] + left_map[1]
-            else:
-                left_map[...] = recv[0, 0:2]
-                right_map[0] = eye
-                right_map[1] = zero
-                right_map[2] = zero
-                right_map[3] = zero
+                joined(other, mine, store_total, (
+                    None, functools.partial(arrive, 0, 1), functools.partial(settle, 0, 1)))
+            new = product(left_map[0], pair(other(0), other(1)))
+            left_map[0] = new[:, :w]
+            left_map[1] = new[:, w:] + left_map[1]
 
     r = rounds - 2
 
@@ -389,9 +428,12 @@
         @pl.when(neighbours[i][0])
         def _(i=i):
             halos[i].wait_send()
-    swap(0).wait_send()
-    swap(1).wait_send()
-    for r in range(1, rounds - 2):
+    for m in range(4):
+        swap(m).wait_send()
+    for k in range(2):
+        give(1, 1, k).wait_send()
+        hand(1, 1, k).wait_send()
+    for r in range(2, rounds - 2):
         for side in range(2):
             @pl.when(bit_of(r) == side)
             def _(r=r, side=side):

time: 34.2 us -> 32.7 us (0.956)
  Pallas kernels: 31.7 us -> 30.5 us
    pallas_call x1, Pallas kernels: 31.7 us -> 30.5 us  [body(): pl.pallas_call(functools.partial(kernel, n_front, n_lat), out_shape=(pltp...]
where the time goes in v6:
time: 32.7 us; the launch traced here: 32.4 us
  Pallas kernels  30.5 us (93%)
  local copies, waits for them, and re-layouts  1.27 us (4%)
  between operations  0.64 us (2%)
    pallas_call x1, Pallas kernels, body(): pl.pallas_call(functools.partial(kernel, n_front, n_lat), out_shape=(pltp...  30.5 us
    unnamed x2, local copies, waits for them, and re-layouts  1.27 us

profile of v6, /device:TPU:0, one launch (start us, length us, event | category | flops | bytes accessed | tf_op | source)
XLA Modules:
  0.0 32.4 jit_solution(5158757603776424886)
XLA Ops:
  0.6 30.5 %shard_map.77 = (f32[16,16,128]{2,1,0:T(8,128)S(1)}, f32[3,16,16]{2,1,0:T(8,128)S(1)}) custom-call(f32[16,16,128]{2,1,0:T(8,128)} %samples_in.1, f32[16,16]{1,0:T(8,128)} %reaction_in.1, f32[16,16]{1,0:T(8,128)} %weight_x_in.1, f32[16,16]{1,0:T(8,128)} %weight_y_in.1, f32[1,2,128,128]{3,2,1,0:T(8,128)} %inverses_in.1, f32[1,2,128,128]{3,2,1,0:T(8,128)} %couplings_in.1), custom_call_target="tpu_custom_call" | custom-call | tf_op jit(solution)/shard_map/pallas_call | solution.py:462
  31.1 0.7 %copy.10 = f32[16,16,128]{2,1,0:T(8,128)} copy(f32[16,16,128]{2,1,0:T(8,128)S(1)} %get-tuple-element.2) | data formatting | bytes 262144
  31.8 0.6 %copy.11 = f32[3,16,16]{2,1,0:T(8,128)} copy(f32[3,16,16]{2,1,0:T(8,128)S(1)} %get-tuple-element.3) | data formatting | bytes 6144

commit v7 on v6

--- a/solution.py
+++ b/solution.py
@@ -164,34 +164,54 @@
         return remote(piece(total, r, kind, core), piece(recv, r, kind, core),
                       sends.at[r, 1], recvs.at[r, core], (front + step, lat))
 
-    def send(r, part):
-        if r == rounds - 2:
-            if part == 0:
-                @pl.when(quarter(0))
-                def _():
-                    direct(r, 0, core).start()
-
-                @pl.when(quarter(2))
-                def _():
-                    give(r, 0, 0).start()
-            else:
-                @pl.when(quarter(3))
-                def _():
-                    direct(r, 1, core).start()
-
-            @pl.when(quarter(1) & (core == part))
+    def sent(r, m):
+        if r < rounds - 2:
+            @pl.when(core == m // 2)
             def _():
-                give(r, 1, 0, part).start()
-                give(r, 1, 1, part).start()
+                give(r, 1, m % 2, m // 2).start()
+            return
+
+        @pl.when(quarter(1) & (core == m // 2))
+        def _():
+            give(r, 1, m % 2, m // 2).start()
+
+        if m == 1:
+            @pl.when(quarter(0))
+            def _():
+                direct(r, 0, core).start()
+
+        if m < 2:
+            @pl.when(quarter(2) & (core == m))
+            def _():
+                give(r, 0, 0, m).start()
         else:
-            @pl.when(bit_of(r) == 0)
+            @pl.when(quarter(3) & (core == m - 2))
             def _():
-                give(r, 0, part).start()
-
-            @pl.when((bit_of(r) == 1) & (core == part))
-            def _():
-                give(r, 1, 0, part).start()
-                give(r, 1, 1, part).start()
+                direct(r, 1, m - 2).start()
+
+    def matrices(r, earlier, later):
+        start = earlier[r, 0]
+        both = product(jnp.concatenate([later[r, 0], later[r, 2]], 0), start)
+        total[r + 1, 0] = both[:w]
+        sent(r + 1, 0)
+        total[r + 1, 2] = earlier[r, 2] + product(start, both[w:], True)
+        sent(r + 1, 2)
+
+    def vectors(r, earlier, later):
+        both = product(jnp.concatenate([later[r, 0], later[r, 2]], 0), earlier[r, 1])
+        total[r + 1, 1] = both[:w] + later[r, 1]
+        sent(r + 1, 1)
+        total[r + 1, 3] = earlier[r, 3] + product(earlier[r, 0], both[w:] + later[r, 3], True)
+        sent(r + 1, 3)
+
+    def merge(step, r):
+        @pl.when(bit_of(r) == 0)
+        def _():
+            step(r, total, recv)
+
+        @pl.when(bit_of(r) == 1)
+        def _():
+            step(r, recv, total)
 
     full = product(t1, t0)
     maps[1] = full
@@ -204,39 +224,9 @@
     tails[0] = inv1
     tails[1] = tail
 
-    def first_matrices(earlier, later):
-        start = earlier[0, 0]
-        both = product(jnp.concatenate([later[0, 0], later[0, 2]], 0), start)
-        total[1, 0] = both[:w]
-        total[1, 2] = earlier[0, 2] + product(start, both[w:], True)
-
-    def first_vectors(earlier, later):
-        both = product(jnp.concatenate([later[0, 0], later[0, 2]], 0), earlier[0, 1])
-        total[1, 1] = both[:w] + later[0, 1]
-
-        @pl.when(core == 0)
-        def _():
-            give(1, 1, 1, 0).start()
-
-        total[1, 3] = earlier[0, 3] + product(earlier[0, 0], both[w:] + later[0, 3], True)
-
-        @pl.when(core == 1)
-        def _():
-            give(1, 1, 1, 1).start()
-
-    def first(step):
-        @pl.when(core == 0)
-        def _():
-            step(total, recv)
-
-        @pl.when(core == 1)
-        def _():
-            step(recv, total)
-
     swap(0).wait_recv()
     swap(2).wait_recv()
-    first(first_matrices)
-    give(1, 1, 0).start()
+    merge(matrices, 0)
     for i, landing in enumerate((halo_x.at[0], halo_x.at[1], halo_y.at[0], halo_y.at[1])):
         comes = neighbours[i ^ 1][0]
 
@@ -268,7 +258,7 @@
     swap(3).start()
     swap(1).wait_recv()
     swap(3).wait_recv()
-    first(first_vectors)
+    merge(vectors, 0)
     eye = (lax.broadcasted_iota(jnp.int32, (w, w), 0) == lax.broadcasted_iota(jnp.int32, (w, w), 1)).astype(F32)
     zero = jnp.zeros((w, w), F32)
 
@@ -286,79 +276,45 @@
         right_map[2] = zero
         right_map[3] = zero
 
-    def joined(earlier, later, store, needs=(None, None, None)):
-        wait = lambda i: needs[i]() if needs[i] else None
-        start = earlier(0)
-        ab = pair(start, earlier(1))
-        both = product(jnp.concatenate([later(0), later(2)], 0), ab)
-        wait(0)
-        store(0, both[:w, :w], both[:w, w:] + later(1))
-        wait(1)
-        mid = pair(both[w:, :w], both[w:, w:] + later(3))
-        new = product(start, mid, True)
-        wait(2)
-        store(1, earlier(2) + new[:, :w], earlier(3) + new[:, w:])
-
-    def store_right(part, first, second):
-        right_map[2 * part] = first
-        right_map[2 * part + 1] = second
-
-    for r in range(1, rounds - 2):
-        def store_total(part, first, second, r=r):
-            total[r + 1, 2 * part] = first
-            total[r + 1, 2 * part + 1] = second
-            send(r + 1, part)
-
-        mine = lambda i, r=r: total[r, i]
-        other = lambda i, r=r: recv[r, i]
-
-        def arrive(side, k, r=r):
-            give(r, side, k).wait_recv()
-            hand(r, side, k).start()
-
-        def settle(side, k, r=r):
-            hand(r, side, k, 1 - core).wait_recv()
-
-        @pl.when(bit_of(r) == 0)
-        def _():
-            def rest():
-                arrive(1, 1)
-                settle(1, 1)
-
-            arrive(1, 0)
-            settle(1, 0)
-            joined(mine, other, store_total, (rest, None, None))
-            joined(lambda i: right_map[i], other, store_right)
-
-        @pl.when(bit_of(r) == 1)
-        def _():
-            if r == 1:
-                for k in range(2):
-                    arrive(1, k)
-                    settle(1, k)
-                joined(other, mine, store_total)
-            else:
-                arrive(0, 0)
-                settle(0, 0)
-                joined(other, mine, store_total, (
-                    None, functools.partial(arrive, 0, 1), functools.partial(settle, 0, 1)))
-            new = product(left_map[0], pair(other(0), other(1)))
-            left_map[0] = new[:, :w]
-            left_map[1] = new[:, w:] + left_map[1]
-
-    r = rounds - 2
-
-    def quarter_arrive(side, k):
+    def extend_right(other):
+        start = right_map[0]
+        ab = pair(start, right_map[1])
+        both = product(jnp.concatenate([other[0], other[2]], 0), ab)
+        right_map[0] = both[:w, :w]
+        right_map[1] = both[:w, w:] + other[1]
+        new = product(start, pair(both[w:, :w], both[w:, w:] + other[3]), True)
+        right_map[2] = right_map[2] + new[:, :w]
+        right_map[3] = right_map[3] + new[:, w:]
+
+    def take(r, side, k):
         give(r, side, k).wait_recv()
         hand(r, side, k).start()
         hand(r, side, k, 1 - core).wait_recv()
 
+    for r in range(1, rounds - 2):
+        take(r, 1, 0)
+        merge(matrices, r)
+        take(r, 1, 1)
+        merge(vectors, r)
+
+        @pl.when(bit_of(r) == 0)
+        def _(r=r):
+            extend_right(recv.at[r])
+
+        @pl.when(bit_of(r) == 1)
+        def _(r=r):
+            new = product(left_map[0], pair(recv[r, 0], recv[r, 1]))
+            left_map[0] = new[:, :w]
+            left_map[1] = new[:, w:] + left_map[1]
+
+    r = rounds - 2
+
     @pl.when(quarter(0))
     def _():
-        quarter_arrive(1, 0)
-        quarter_arrive(1, 1)
+        take(r, 1, 0)
+        take(r, 1, 1)
         total[r + 1, 1] = product(recv[r, 0], total[r, 1]) + recv[r, 1]
-        joined(lambda i: right_map[i], lambda i: recv[r, i], store_right)
+        extend_right(recv.at[r])
 
     @pl.when(quarter(1))
     def _():
@@ -386,7 +342,7 @@
 
     @pl.when(quarter(3))
     def _():
-        quarter_arrive(0, 0)
+        take(r, 0, 0)
         new = product(left_map[0], pair(recv[r, 0], recv[r, 1]))
         left_map[0] = new[:, :w]
         left_map[1] = new[:, w:] + left_map[1]
@@ -430,16 +386,10 @@
             halos[i].wait_send()
     for m in range(4):
         swap(m).wait_send()
-    for k in range(2):
-        give(1, 1, k).wait_send()
-        hand(1, 1, k).wait_send()
-    for r in range(2, rounds - 2):
-        for side in range(2):
-            @pl.when(bit_of(r) == side)
-            def _(r=r, side=side):
-                for k in range(2):
-                    give(r, side, k).wait_send()
-                    hand(r, 1 - side, k).wait_send()
+    for r in range(1, rounds - 2):
+        for k in range(2):
+            give(r, 1, k).wait_send()
+            hand(r, 1, k).wait_send()
     r, z = rounds - 2, rounds - 1
     for p, started in enumerate((
         (direct(r, 0, core), hand(r, 1, 0), hand(r, 1, 1)),

time: 32.7 us -> 30.3 us (0.927)
  the two profiles are of different devices: /device:TPU:0 before, /device:TPU:1 now
where the time goes in v7:
time: 30.3 us; the launch traced here: 30.1 us
  Pallas kernels  28.2 us (93%)
  local copies, waits for them, and re-layouts  1.27 us (4%)
  between operations  0.64 us (2%)
    pallas_call x1, Pallas kernels, body(): pl.pallas_call(functools.partial(kernel, n_front, n_lat), out_shape=(pltp...  28.2 us
    unnamed x2, local copies, waits for them, and re-layouts  1.27 us

profile of v7, /device:TPU:1, one launch (start us, length us, event | category | flops | bytes accessed | tf_op | source)
XLA Modules:
  0.0 30.1 jit_solution(10917854997312243379)
XLA Ops:
  0.6 28.2 %shard_map.77 = (f32[16,16,128]{2,1,0:T(8,128)S(1)}, f32[3,16,16]{2,1,0:T(8,128)S(1)}) custom-call(f32[16,16,128]{2,1,0:T(8,128)} %samples_in.1, f32[16,16]{1,0:T(8,128)} %reaction_in.1, f32[16,16]{1,0:T(8,128)} %weight_x_in.1, f32[16,16]{1,0:T(8,128)} %weight_y_in.1, f32[1,2,128,128]{3,2,1,0:T(8,128)} %inverses_in.1, f32[1,2,128,128]{3,2,1,0:T(8,128)} %couplings_in.1), custom_call_target="tpu_custom_call" | custom-call | tf_op jit(solution)/shard_map/pallas_call | solution.py:412
  28.8 0.7 %copy.10 = f32[16,16,128]{2,1,0:T(8,128)} copy(f32[16,16,128]{2,1,0:T(8,128)S(1)} %get-tuple-element.2) | data formatting | bytes 262144
  29.5 0.6 %copy.11 = f32[3,16,16]{2,1,0:T(8,128)} copy(f32[3,16,16]{2,1,0:T(8,128)S(1)} %get-tuple-element.3) | data formatting | bytes 6144

commit v8 on v7

--- a/solution.py
+++ b/solution.py
@@ -328,14 +328,31 @@
         mid = product(recv[r, 2], pair(a, b))
         return product(a, pair(mid[:, :w], mid[:, w:] + recv[r, 3]), True)
 
+    def one(r, which):
+        @pl.when(core == which)
+        def _():
+            direct(r, 1, which).wait_recv()
+            relay(r, 1, which).start()
+
+        @pl.when(core != which)
+        def _():
+            relay(r, 1, which).wait_recv()
+
+    def give_back(which):
+        @pl.when(core == which)
+        def _():
+            direct(rounds - 1, 1, which).start()
+            near(1).start()
+
     @pl.when(quarter(2))
     def _():
-        receive(r, 1)
-        new = adjoint(total[r, 0], total[r, 1])
-        total[r + 1, 2] = total[r, 2] + new[:, :w]
-        total[r + 1, 3] = total[r, 3] + new[:, w:]
-        direct(r + 1, 1, core).start()
-        near(1).start()
+        one(r, 0)
+        mid = product(recv[r, 2], pair(total[r, 0], total[r, 1]))
+        total[r + 1, 2] = total[r, 2] + product(total[r, 0], mid[:, :w], True)
+        give_back(0)
+        one(r, 1)
+        total[r + 1, 3] = total[r, 3] + product(total[r, 0], mid[:, w:] + recv[r, 3], True)
+        give_back(1)
         new = adjoint(right_map[0], right_map[1])
         right_map[2] = right_map[2] + new[:, :w]
         right_map[3] = right_map[3] + new[:, w:]
@@ -363,8 +380,10 @@
     def _():
         x1, x0 = finish(values[...].reshape(2 * w, count) + product(stack, left_map[1]))
         back = product(right_map[0], tail)
-        receive(z, 1)
-        middle = product(recv[z, 2], total[z, 1]) + recv[z, 3]
+        one(z, 0)
+        middle = product(recv[z, 2], total[z, 1])
+        one(z, 1)
+        middle = middle + recv[z, 3]
         change = product(back, middle, True)
         put(x1 - change[:w], x0 - change[w:])
 

time: 30.3 us -> 29.9 us (0.987)
  the two profiles are of different devices: /device:TPU:1 before, /device:TPU:0 now
where the time goes in v8:
time: 29.9 us; the launch traced here: 29.8 us
  Pallas kernels  27.9 us (93%)
  local copies, waits for them, and re-layouts  1.27 us (4%)
  between operations  0.64 us (2%)
    pallas_call x1, Pallas kernels, body(): pl.pallas_call(functools.partial(kernel, n_front, n_lat), out_shape=(pltp...  27.9 us
    unnamed x2, local copies, waits for them, and re-layouts  1.27 us

profile of v8, /device:TPU:0, one launch (start us, length us, event | category | flops | bytes accessed | tf_op | source)
XLA Modules:
  0.0 29.8 jit_solution(16134422173521003119)
XLA Ops:
  0.6 27.9 %shard_map.77 = (f32[16,16,128]{2,1,0:T(8,128)S(1)}, f32[3,16,16]{2,1,0:T(8,128)S(1)}) custom-call(f32[16,16,128]{2,1,0:T(8,128)} %samples_in.1, f32[16,16]{1,0:T(8,128)} %reaction_in.1, f32[16,16]{1,0:T(8,128)} %weight_x_in.1, f32[16,16]{1,0:T(8,128)} %weight_y_in.1, f32[1,2,128,128]{3,2,1,0:T(8,128)} %inverses_in.1, f32[1,2,128,128]{3,2,1,0:T(8,128)} %couplings_in.1), custom_call_target="tpu_custom_call" | custom-call | tf_op jit(solution)/shard_map/pallas_call | solution.py:431
  28.5 0.7 %copy.10 = f32[16,16,128]{2,1,0:T(8,128)} copy(f32[16,16,128]{2,1,0:T(8,128)S(1)} %get-tuple-element.2) | data formatting | bytes 262144
  29.2 0.6 %copy.11 = f32[3,16,16]{2,1,0:T(8,128)} copy(f32[3,16,16]{2,1,0:T(8,128)S(1)} %get-tuple-element.3) | data formatting | bytes 6144
